TPU v7x, 32 devices: a whole 2x2x4 slice. The times are simulated.
32 devices in a mesh: group: 2 (over y), store: 4 (over z), tensor: 2 (over x), rep: 2 (over core).
Axes of the slice: x: 2, y: 2, z: 4, core: 2. Of those that a mesh axis runs over, the one named last changes fastest.
Arguments:
- queries: bfloat16 [8, 256, 4096], P(('group', 'store'), 'rep', 'tensor'), parts along dimension 0, may hold values from -40 to 40
- hidden: bfloat16 [8, 256, 7168], P(('group', 'store'), 'rep', 'tensor'), parts along dimension 0, may hold values from -6 to 6
- key_value_weight: bfloat16 [7168, 1024], P(('tensor', 'rep')), may hold values from -0.0625 to 0.0625
- page_store: bfloat16 [256, 2, 128, 512], P(('group', 'store'), None, None, 'tensor'), parts along dimension 0, may hold values from -30 to 30
- prefix_holder: int32 [8, 64, 1], P('group'), parts along dimension 0, may hold values from 0 to 3; in each aligned block of 32 rows (0 to 31, 32 to 63, ..., all dimensions but the last counted through in order) at most 8 rows name the same one
- prefix_slot: int32 [8, 64], P('group'), parts along dimension 0, may hold values from 0 to 31
- prefix_len: int32 [8], P('group'), parts along dimension 0, may hold values from 1 to 8192, 26214 in all
- new_owner: int32 [2, 8], P(None, 'group'), parts along dimension 1, may hold values from 0 to 3, each once within a row
Outputs:
- attended: bfloat16 [8, 256, 4096], P(('group', 'store'), 'rep', 'tensor'), parts along dimension 0
- added_pages: bfloat16 [8, 2, 2, 128, 512], P(('group', 'store'), 'rep', None, None, 'tensor'), parts along dimension 0
There are 2 independent parts, one for each index of `group`. A program takes and returns all parts, laid end to end along the dimension named above; an argument that names none is the same for every part. Nothing has to cross between parts.
Inputs may be any that keep to these rules, and one draw needn't show every extreme that they name: `prefix_holder`: within each half of one request's list (32 entries in order) no holder is named more than 8 times. The entry names row prefix_holder * 32 + prefix_slot of the group's page store. `new_owner`: each row is a permutation of the store indices.
All inputs are finite; a program needn't handle non-finite values.
Results may differ from a plain program's by a relative error of at most 0.02.
Values may be sent and summed in bfloat16 or wider, within the bound.
A program may use at most 128 MiB of HBM per device.

v0:
```python
import math

import jax
import jax.numpy as jnp
from jax import lax
from jax.sharding import PartitionSpec as P

HEAD_ENTRIES = 128


NEG_FILL = -1e30


def from_behind(block, axis, distance):
    devices = range(lax.axis_size(axis))
    route = [(i - distance, i) for i in devices if i - distance in devices]
    return lax.ppermute(block, axis, route)


def attend_block(running, query_matrix, key_rows, values, allowed):
    row_max, weight_sum, weighted = running
    score_scale = 1.0 / math.sqrt(key_rows.shape[-1])
    scores = (
        jnp.einsum("rhgd,khd->hgrk", query_matrix, key_rows, preferred_element_type=jnp.float32)
        * score_scale
    )
    scores = jnp.where(allowed, scores, NEG_FILL)
    fresh_max = jnp.maximum(row_max, jnp.max(scores, axis=-1))
    shrink = jnp.exp(row_max - fresh_max)
    weights = jnp.where(allowed, jnp.exp(scores - fresh_max[..., None]), 0.0)
    weight_sum = weight_sum * shrink + jnp.sum(weights, axis=-1)
    weighted = weighted * shrink[..., None] + jnp.einsum(
        "hgrk,khd->hgrd", weights.astype(jnp.bfloat16), values, preferred_element_type=jnp.float32
    )
    return (fresh_max, weight_sum, weighted)


def start_carry(kv_heads, serving_groups, row_count, head_size):
    return (
        jnp.full((kv_heads, serving_groups, row_count), NEG_FILL, jnp.float32),
        jnp.zeros((kv_heads, serving_groups, row_count), jnp.float32),
        jnp.zeros((kv_heads, serving_groups, row_count, head_size), jnp.float32),
    )


def scan_pages(running, query_matrix, pulled, token_ok):
    page_count = pulled.shape[0]
    page_len = pulled.shape[2]
    kv_heads = query_matrix.shape[1]
    head_size = query_matrix.shape[3]
    per_block = math.gcd(page_count, max(1, 1024 // page_len))
    blocks = page_count // per_block
    page_blocks = pulled.reshape(blocks, per_block, 2, page_len, kv_heads, head_size)
    ok_blocks = token_ok.reshape(blocks, per_block * page_len)

    def visit_block(state_now, block_item):
        page_block, block_ok = block_item
        key_rows = page_block[:, 0].reshape(per_block * page_len, kv_heads, head_size)
        values = page_block[:, 1].reshape(per_block * page_len, kv_heads, head_size)
        return (
            attend_block(state_now, query_matrix, key_rows, values, block_ok[None, None, None, :]),
            None,
        )

    running, unused = lax.scan(visit_block, running, (page_blocks, ok_blocks))
    return running


def pull_plan(holders, places):
    member = (holders[:, :, None] == jnp.arange(places, dtype=jnp.int32)[None, None, :]).astype(
        jnp.int32
    )
    ranking = jnp.sum((jnp.cumsum(member, axis=1) - 1) * member, axis=-1)
    return (holders, ranking)


def send_pages(page_store, holders_part, ranking, slots, capacity, store_id):
    chosen = (holders_part == store_id)[:, None, :] & (
        ranking[:, None, :] == jnp.arange(capacity, dtype=jnp.int32)[None, :, None]
    )
    slot_of = jnp.sum(jnp.where(chosen, slots[:, None, :], 0), axis=-1)
    return page_store[slot_of.reshape(-1)]


def receive_order(received, holders_part, ranking, store_id, capacity):
    own_holders = lax.dynamic_index_in_dim(holders_part, store_id, 0, keepdims=False)
    my_rank = lax.dynamic_index_in_dim(ranking, store_id, 0, keepdims=False)
    return received[own_holders * capacity + my_rank]


def shards(
    queries, hidden, key_value_weight, page_store, prefix_holder, prefix_slot, prefix_len, new_owner
):
    store_id = lax.axis_index("store")
    rep_id = lax.axis_index("rep")
    stores = lax.axis_size("store")
    tensors = lax.axis_size("tensor")
    tokens = queries.shape[1]
    page_len = page_store.shape[2]
    local_width = page_store.shape[3]
    kv_heads = local_width // HEAD_ENTRIES
    serving_groups = queries.shape[2] // local_width
    quarter_rows = hidden.shape[2]
    own_rows = hidden[0]
    weight_full = lax.all_gather(key_value_weight, "rep", axis=0, tiled=True)
    weight_five = weight_full.reshape(quarter_rows, tensors, kv_heads, 2, HEAD_ENTRIES)
    partial_value = jnp.einsum(
        "tc,cghkd->gkthd", own_rows, weight_five, preferred_element_type=jnp.float32
    )
    summed = lax.psum_scatter(
        partial_value.reshape(tensors * 2 * tokens, kv_heads * HEAD_ENTRIES).astype(jnp.bfloat16),
        "tensor",
        scatter_dimension=0,
        tiled=True,
    )
    own_kv = summed.reshape(2, tokens, kv_heads * HEAD_ENTRIES)
    spread = lax.all_gather(own_kv[None], "store", axis=0, tiled=True)
    owner_row = lax.dynamic_index_in_dim(new_owner, rep_id, 0, keepdims=False)
    owner_pick = (owner_row == store_id).astype(jnp.bfloat16)
    new_page = jnp.einsum(
        "n,nktc->ktc", owner_pick, spread, preferred_element_type=jnp.float32
    ).astype(jnp.bfloat16)
    added_pages = new_page.reshape(1, 1, 2, tokens, kv_heads * HEAD_ENTRIES)
    earlier = from_behind(own_kv, "rep", 1)
    new_keys = jnp.concatenate([earlier[0], own_kv[0]], 0).reshape(
        2 * tokens, kv_heads, HEAD_ENTRIES
    )
    new_values = jnp.concatenate([earlier[1], own_kv[1]], 0).reshape(
        2 * tokens, kv_heads, HEAD_ENTRIES
    )
    key_index = jnp.arange(2 * tokens, dtype=jnp.int32)[None, :]
    query_index = jnp.arange(tokens, dtype=jnp.int32)[:, None]
    allowed_new = jnp.where(key_index < tokens, rep_id > 0, key_index - tokens <= query_index)
    my_len = lax.dynamic_index_in_dim(prefix_len, store_id, 0, keepdims=False)
    list_len = prefix_slot.shape[1]
    holders = prefix_holder[:, :, 0]
    query_matrix = queries[0].reshape(tokens, kv_heads, serving_groups, HEAD_ENTRIES)
    capacity = 2 * max(2, list_len // (2 * stores))
    holders_part, ranking = pull_plan(holders, stores)
    outgoing = send_pages(page_store, holders_part, ranking, prefix_slot, capacity, store_id)
    incoming = lax.all_to_all(outgoing, "store", split_axis=0, concat_axis=0, tiled=True)
    pulled = receive_order(incoming, holders_part, ranking, store_id, capacity)
    token_ok = jnp.arange(list_len * page_len, dtype=jnp.int32) < my_len
    running = scan_pages(
        start_carry(kv_heads, serving_groups, tokens, HEAD_ENTRIES), query_matrix, pulled, token_ok
    )
    running = attend_block(running, query_matrix, new_keys, new_values, allowed_new[None, None])
    row_max, weight_sum, weighted = running
    result = (
        (weighted / weight_sum[..., None])
        .transpose(2, 0, 1, 3)
        .reshape(1, tokens, kv_heads * serving_groups * HEAD_ENTRIES)
    )
    return (result.astype(jnp.bfloat16), added_pages)


def solution(mesh):
    placed = (
        P(("group", "store"), "rep", "tensor"),
        P(("group", "store"), "rep", "tensor"),
        P(("tensor", "rep"), None),
        P(("group", "store"), None, None, "tensor"),
        P("group", None, None),
        P("group", None),
        P("group"),
        P(None, "group"),
    )
    return jax.shard_map(
        shards,
        mesh=mesh,
        in_specs=placed,
        out_specs=(
            P(("group", "store"), "rep", "tensor"),
            P(("group", "store"), "rep", None, None, "tensor"),
        ),
        check_vma=False,
    )
```

profile of v0, /device:TPU:8, one launch (start us, length us, event | category | flops | bytes accessed | tf_op | source)
XLA Modules:
  0.0 389.1 jit_solution(3936829598589900630)
XLA Ops:
  10.7 7.7 %gather_fusion = bf16[64,2,128,256]{3,2,1,0:T(8,128)(2,1)} fusion(bf16[32,2,128,256]{3,2,1,0:T(8,128)(2,1)} %param.13, s32[1024]{0:T(1024)S(1)} %pad_clamp_fusion.1), kind=kCustom, calls=%fused_computation | custom fusion | bytes 16777472 | tf_op jit(solution)/shard_map/gather | solution.py:82
  18.4 5.7 %all-to-all-start = ((bf16[64,2,128,256]{3,2,1,0:T(8,128)(2,1)}), bf16[64,2,128,256]{3,2,1,0:T(8,128)(2,1)}, u32[]{:S(2)}, u32[]{:S(2)}) async-start(bf16[64,2,128,256]{3,2,1,0:T(8,128)(2,1)} %gather_fusion), calls=%async_computation | async-start | bytes 16777216 | tf_op jit(solution)/shard_map/all_to_all | solution.py:141
  26.8 19.7 %all-gather.2.cloned.1.call-done = bf16[3584,1024]{1,0:T(8,128)(2,1)} async-done(((bf16[1792,1024]{1,0:T(8,128)(2,1)}), bf16[3584,1024]{1,0:T(8,128)(2,1)}) %all-gather.2.cloned.1.call-update) | async-done | bytes 7340048 | tf_op jit(solution)/shard_map/all_gather | solution.py:105
  46.5 10.0 %copy.68 = bf16[3584,1024]{0,1:T(8,128)(2,1)} copy(bf16[3584,1024]{1,0:T(8,128)(2,1)} %all-gather.2.cloned.1.call-done) | data formatting | bytes 14680064 | tf_op jit(solution)/shard_map/all_gather | solution.py:105
  56.6 5.1 %fusion.20 = bf16[2,2,128,2,128]{2,4,1,3,0:T(8,128)(2,1)S(1)} fusion(bf16[3584,2,2,2,128]{0,4,3,2,1:T(8,128)(2,1)} %bitcast.134, bf16[1,128,3584]{2,1,0:T(8,128)(2,1)S(1)} %copy-done), kind=kOutput, calls=%fused_computation.32 | convolution fusion | flops 939655168 | bytes 8519680 | tf_op jit(solution)/shard_map/tc,cghkd->gkthd/dot_general | solution.py:107
  63.5 11.9 %reduce-scatter.2.cloned.1.call-done = bf16[256,256]{1,0:T(8,128)(2,1)} async-done(((bf16[512,256]{1,0:T(8,128)(2,1)}), bf16[256,256]{1,0:T(8,128)(2,1)}) %reduce-scatter.2.cloned.1.call-update) | async-done | bytes 131088 | tf_op jit(solution)/shard_map/reduce_scatter | solution.py:110
  75.4 1.0 copy.70
  76.4 1.7 collective-permute-start
  80.0 137.7 %all_gather.7 = bf16[4,2,128,256]{3,2,1,0:T(8,128)(2,1)S(1)} all-gather(bf16[1,2,128,256]{3,2,1,0:T(8,128)(2,1)} %bitcast.138), channel_id=1, replica_groups=mesh['group'=2,'store'=4,'tensor'=2,'rep'=2] {'store'}, dimensions={0}, use_global_device_ids=true | all-gather | bytes 655360 | tf_op jit(solution)/shard_map/all_gather | solution.py:117
  219.7 2.4 fusion.15
  222.1 8.9 %gather_fusion.1 = bf16[64,2,128,256]{3,2,1,0:T(8,128)(2,1)} fusion(bf16[64,2,128,256]{3,2,1,0:T(8,128)(2,1)} %all-to-all-done, s32[1024]{0:T(1024)S(1)} %pad_clamp_fusion), kind=kCustom, calls=%fused_computation.1 | custom fusion | bytes 16777472 | tf_op jit(solution)/shard_map/gather | solution.py:88
  231.0 11.9 %copy.64 = bf16[64,2,128,256]{2,3,1,0:T(8,128)(2,1)} copy(bf16[64,2,128,256]{3,2,1,0:T(8,128)(2,1)} %gather_fusion.1) | data formatting | bytes 16777216 | tf_op jit(solution)/shard_map/gather | solution.py:88
  242.9 131.5 %while.15 = (s32[]{:T(128)}, f32[2,8,128]{2,1,0:T(8,128)S(1)}, f32[2,8,128]{2,1,0:T(8,128)S(1)}, f32[2,8,128,128]{3,2,1,0:T(8,128)}, pred[8,1024]{1,0:T(8,128)(4...) while((s32[]{:T(128)}, f32[2,8,128]{2,1,0:T(8,128)S(1)}, ...), condition=%wide.region_6.7_spmd.clone, body=%wide.region_3.6_spmd.clone.sunk | while | flops 1101801472 | bytes 77206728 | solution.py:65
  242.9 1.3 constant_dynamic-slice_fusion.6
  245.0 4.1 %bitcast_reduce_fusion.2 = (f32[2,8,128]{2,1,0:T(8,128)S(1)}, f32[2,1024,128,8]{2,1,3,0:T(8,128)}) fusion(pred[1024]{0:T(1024)(128)(4,1)S(1)} %dynamic-slice_reduce_fusion.2, bf16[1024,2,128,1]{2,0,3,1:T(8,128)(2,1)S(1)} %bitcast.131, bf16[128,2,8,128]{3,0,2,1:T(8,128)(2,1)S(1)} %get-tuple-element.213), kind=kOutput, calls=%fused_computation.3.clone.1 | convolution fusion | flops 543160320 | bytes 9446400 | tf_op jit(solution)/shard_map/while/body/eval_jaxpr/rhgd,khd->hgrk/dot_general | solution.py:24
  249.1 4.8 %fusion.72 = f32[2,8,128]{2,1,0:T(8,128)S(1)} fusion(f32[2,1024,128,8]{2,1,3,0:T(8,128)} %get-tuple-element.185, f32[2,8,128]{2,1,0:T(8,128)S(1)} %select_maximum_fusion.2, pred[1024]{0:T(1024)(128)(4,1)S(1)} %dynamic-slice_reduce_fusion.2), kind=kLoop, calls=%fused_computation.8.clone.1 | loop fusion | flops 10483712 | bytes 8406016 | tf_op jit(solution)/shard_map/while/body/eval_jaxpr/reduce_sum | solution.py:31
  253.9 1.0 copy-done.2
  254.9 3.4 fusion.74
  258.4 1.0 copy-done.4
  259.4 1.3 constant_dynamic-slice_fusion.6
  261.4 4.1 %bitcast_reduce_fusion.2 = (f32[2,8,128]{2,1,0:T(8,128)S(1)}, f32[2,1024,128,8]{2,1,3,0:T(8,128)}) fusion(pred[1024]{0:T(1024)(128)(4,1)S(1)} %dynamic-slice_reduce_fusion.2, bf16[1024,2,128,1]{2,0,3,1:T(8,128)(2,1)S(1)} %bitcast.131, bf16[128,2,8,128]{3,0,2,1:T(8,128)(2,1)S(1)} %get-tuple-element.213), kind=kOutput, calls=%fused_computation.3.clone.1 | convolution fusion | flops 543160320 | bytes 9446400 | tf_op jit(solution)/shard_map/while/body/eval_jaxpr/rhgd,khd->hgrk/dot_general | solution.py:24
  265.5 4.8 %fusion.72 = f32[2,8,128]{2,1,0:T(8,128)S(1)} fusion(f32[2,1024,128,8]{2,1,3,0:T(8,128)} %get-tuple-element.185, f32[2,8,128]{2,1,0:T(8,128)S(1)} %select_maximum_fusion.2, pred[1024]{0:T(1024)(128)(4,1)S(1)} %dynamic-slice_reduce_fusion.2), kind=kLoop, calls=%fused_computation.8.clone.1 | loop fusion | flops 10483712 | bytes 8406016 | tf_op jit(solution)/shard_map/while/body/eval_jaxpr/reduce_sum | solution.py:31
  270.3 1.0 copy-done.2
  271.3 3.4 fusion.74
  274.8 1.0 copy-done.4
  275.8 1.3 constant_dynamic-slice_fusion.6
  277.9 4.1 %bitcast_reduce_fusion.2 = (f32[2,8,128]{2,1,0:T(8,128)S(1)}, f32[2,1024,128,8]{2,1,3,0:T(8,128)}) fusion(pred[1024]{0:T(1024)(128)(4,1)S(1)} %dynamic-slice_reduce_fusion.2, bf16[1024,2,128,1]{2,0,3,1:T(8,128)(2,1)S(1)} %bitcast.131, bf16[128,2,8,128]{3,0,2,1:T(8,128)(2,1)S(1)} %get-tuple-element.213), kind=kOutput, calls=%fused_computation.3.clone.1 | convolution fusion | flops 543160320 | bytes 9446400 | tf_op jit(solution)/shard_map/while/body/eval_jaxpr/rhgd,khd->hgrk/dot_general | solution.py:24
  282.0 4.8 %fusion.72 = f32[2,8,128]{2,1,0:T(8,128)S(1)} fusion(f32[2,1024,128,8]{2,1,3,0:T(8,128)} %get-tuple-element.185, f32[2,8,128]{2,1,0:T(8,128)S(1)} %select_maximum_fusion.2, pred[1024]{0:T(1024)(128)(4,1)S(1)} %dynamic-slice_reduce_fusion.2), kind=kLoop, calls=%fused_computation.8.clone.1 | loop fusion | flops 10483712 | bytes 8406016 | tf_op jit(solution)/shard_map/while/body/eval_jaxpr/reduce_sum | solution.py:31
  286.8 1.0 copy-done.2
  287.8 3.4 fusion.74
  291.3 1.0 copy-done.4
  292.2 1.3 constant_dynamic-slice_fusion.6
  294.3 4.1 %bitcast_reduce_fusion.2 = (f32[2,8,128]{2,1,0:T(8,128)S(1)}, f32[2,1024,128,8]{2,1,3,0:T(8,128)}) fusion(pred[1024]{0:T(1024)(128)(4,1)S(1)} %dynamic-slice_reduce_fusion.2, bf16[1024,2,128,1]{2,0,3,1:T(8,128)(2,1)S(1)} %bitcast.131, bf16[128,2,8,128]{3,0,2,1:T(8,128)(2,1)S(1)} %get-tuple-element.213), kind=kOutput, calls=%fused_computation.3.clone.1 | convolution fusion | flops 543160320 | bytes 9446400 | tf_op jit(solution)/shard_map/while/body/eval_jaxpr/rhgd,khd->hgrk/dot_general | solution.py:24
  298.4 4.8 %fusion.72 = f32[2,8,128]{2,1,0:T(8,128)S(1)} fusion(f32[2,1024,128,8]{2,1,3,0:T(8,128)} %get-tuple-element.185, f32[2,8,128]{2,1,0:T(8,128)S(1)} %select_maximum_fusion.2, pred[1024]{0:T(1024)(128)(4,1)S(1)} %dynamic-slice_reduce_fusion.2), kind=kLoop, calls=%fused_computation.8.clone.1 | loop fusion | flops 10483712 | bytes 8406016 | tf_op jit(solution)/shard_map/while/body/eval_jaxpr/reduce_sum | solution.py:31
  303.2 1.0 copy-done.2
  304.2 3.4 fusion.74
  307.7 1.0 copy-done.4
  308.7 1.3 constant_dynamic-slice_fusion.6
  310.8 4.1 %bitcast_reduce_fusion.2 = (f32[2,8,128]{2,1,0:T(8,128)S(1)}, f32[2,1024,128,8]{2,1,3,0:T(8,128)}) fusion(pred[1024]{0:T(1024)(128)(4,1)S(1)} %dynamic-slice_reduce_fusion.2, bf16[1024,2,128,1]{2,0,3,1:T(8,128)(2,1)S(1)} %bitcast.131, bf16[128,2,8,128]{3,0,2,1:T(8,128)(2,1)S(1)} %get-tuple-element.213), kind=kOutput, calls=%fused_computation.3.clone.1 | convolution fusion | flops 543160320 | bytes 9446400 | tf_op jit(solution)/shard_map/while/body/eval_jaxpr/rhgd,khd->hgrk/dot_general | solution.py:24
  314.8 4.8 %fusion.72 = f32[2,8,128]{2,1,0:T(8,128)S(1)} fusion(f32[2,1024,128,8]{2,1,3,0:T(8,128)} %get-tuple-element.185, f32[2,8,128]{2,1,0:T(8,128)S(1)} %select_maximum_fusion.2, pred[1024]{0:T(1024)(128)(4,1)S(1)} %dynamic-slice_reduce_fusion.2), kind=kLoop, calls=%fused_computation.8.clone.1 | loop fusion | flops 10483712 | bytes 8406016 | tf_op jit(solution)/shard_map/while/body/eval_jaxpr/reduce_sum | solution.py:31
  319.6 1.0 copy-done.2
  320.7 3.4 fusion.74
  324.2 1.0 copy-done.4
  325.1 1.3 constant_dynamic-slice_fusion.6
  327.2 4.1 %bitcast_reduce_fusion.2 = (f32[2,8,128]{2,1,0:T(8,128)S(1)}, f32[2,1024,128,8]{2,1,3,0:T(8,128)}) fusion(pred[1024]{0:T(1024)(128)(4,1)S(1)} %dynamic-slice_reduce_fusion.2, bf16[1024,2,128,1]{2,0,3,1:T(8,128)(2,1)S(1)} %bitcast.131, bf16[128,2,8,128]{3,0,2,1:T(8,128)(2,1)S(1)} %get-tuple-element.213), kind=kOutput, calls=%fused_computation.3.clone.1 | convolution fusion | flops 543160320 | bytes 9446400 | tf_op jit(solution)/shard_map/while/body/eval_jaxpr/rhgd,khd->hgrk/dot_general | solution.py:24
  331.3 4.8 %fusion.72 = f32[2,8,128]{2,1,0:T(8,128)S(1)} fusion(f32[2,1024,128,8]{2,1,3,0:T(8,128)} %get-tuple-element.185, f32[2,8,128]{2,1,0:T(8,128)S(1)} %select_maximum_fusion.2, pred[1024]{0:T(1024)(128)(4,1)S(1)} %dynamic-slice_reduce_fusion.2), kind=kLoop, calls=%fused_computation.8.clone.1 | loop fusion | flops 10483712 | bytes 8406016 | tf_op jit(solution)/shard_map/while/body/eval_jaxpr/reduce_sum | solution.py:31
  336.1 1.0 copy-done.2
  337.1 3.4 fusion.74
  340.6 1.0 copy-done.4
  341.6 1.3 constant_dynamic-slice_fusion.6
  343.7 4.1 %bitcast_reduce_fusion.2 = (f32[2,8,128]{2,1,0:T(8,128)S(1)}, f32[2,1024,128,8]{2,1,3,0:T(8,128)}) fusion(pred[1024]{0:T(1024)(128)(4,1)S(1)} %dynamic-slice_reduce_fusion.2, bf16[1024,2,128,1]{2,0,3,1:T(8,128)(2,1)S(1)} %bitcast.131, bf16[128,2,8,128]{3,0,2,1:T(8,128)(2,1)S(1)} %get-tuple-element.213), kind=kOutput, calls=%fused_computation.3.clone.1 | convolution fusion | flops 543160320 | bytes 9446400 | tf_op jit(solution)/shard_map/while/body/eval_jaxpr/rhgd,khd->hgrk/dot_general | solution.py:24
  347.7 4.8 %fusion.72 = f32[2,8,128]{2,1,0:T(8,128)S(1)} fusion(f32[2,1024,128,8]{2,1,3,0:T(8,128)} %get-tuple-element.185, f32[2,8,128]{2,1,0:T(8,128)S(1)} %select_maximum_fusion.2, pred[1024]{0:T(1024)(128)(4,1)S(1)} %dynamic-slice_reduce_fusion.2), kind=kLoop, calls=%fused_computation.8.clone.1 | loop fusion | flops 10483712 | bytes 8406016 | tf_op jit(solution)/shard_map/while/body/eval_jaxpr/reduce_sum | solution.py:31
  352.5 1.0 copy-done.2
  353.6 3.4 fusion.74
  357.0 1.0 copy-done.4
  358.0 1.3 constant_dynamic-slice_fusion.6
  360.1 4.1 %bitcast_reduce_fusion.2 = (f32[2,8,128]{2,1,0:T(8,128)S(1)}, f32[2,1024,128,8]{2,1,3,0:T(8,128)}) fusion(pred[1024]{0:T(1024)(128)(4,1)S(1)} %dynamic-slice_reduce_fusion.2, bf16[1024,2,128,1]{2,0,3,1:T(8,128)(2,1)S(1)} %bitcast.131, bf16[128,2,8,128]{3,0,2,1:T(8,128)(2,1)S(1)} %get-tuple-element.213), kind=kOutput, calls=%fused_computation.3.clone.1 | convolution fusion | flops 543160320 | bytes 9446400 | tf_op jit(solution)/shard_map/while/body/eval_jaxpr/rhgd,khd->hgrk/dot_general | solution.py:24
  364.2 4.8 %fusion.72 = f32[2,8,128]{2,1,0:T(8,128)S(1)} fusion(f32[2,1024,128,8]{2,1,3,0:T(8,128)} %get-tuple-element.185, f32[2,8,128]{2,1,0:T(8,128)S(1)} %select_maximum_fusion.2, pred[1024]{0:T(1024)(128)(4,1)S(1)} %dynamic-slice_reduce_fusion.2), kind=kLoop, calls=%fused_computation.8.clone.1 | loop fusion | flops 10483712 | bytes 8406016 | tf_op jit(solution)/shard_map/while/body/eval_jaxpr/reduce_sum | solution.py:31
  369.0 1.0 copy-done.2
  370.0 3.4 fusion.74
  374.4 1.6 copy.75
  376.8 2.1 fusion.16
  378.9 2.3 fusion.19
  381.2 1.0 copy.78
  (131 shorter events, 19.8 us)
Async XLA Ops:
  7.2 49.4 %copy-start = (bf16[1,128,3584]{2,1,0:T(8,128)(2,1)S(1)}, bf16[1,128,3584]{2,1,0:T(8,128)(2,1)}, u32[]{:S(2)}) copy-start(bf16[1,128,3584]{2,1,0:T(8,128)(2,1)} %param.11) | copy-start | bytes 2752516
  18.4 6.5 %copy-start.5 = (bf16[1,128,2048]{2,1,0:T(8,128)(2,1)S(1)}, bf16[1,128,2048]{2,1,0:T(8,128)(2,1)}, u32[]{:S(2)}) copy-start(bf16[1,128,2048]{2,1,0:T(8,128)(2,1)} %param.10) | copy-start | bytes 1572868
  18.4 7.1 %copy-start.8 = (s32[4]{0:T(128)S(1)}, s32[4]{0:T(128)}, u32[]{:S(2)}) copy-start(s32[4]{0:T(128)} %param.16) | copy-start | bytes 52
  18.4 203.6 %all-to-all-start = ((bf16[64,2,128,256]{3,2,1,0:T(8,128)(2,1)}), bf16[64,2,128,256]{3,2,1,0:T(8,128)(2,1)}, u32[]{:S(2)}, u32[]{:S(2)}) async-start(bf16[64,2,128,256]{3,2,1,0:T(8,128)(2,1)} %gather_fusion), calls=%async_computation | async-start | bytes 16777216 | tf_op jit(solution)/shard_map/all_to_all | solution.py:141
  24.1 22.4 %all-gather.2.cloned.1.call-start = ((), (), s32[]{:S(2)}) async-start(), calls=%async_computation.2 | async-start | bytes 11010048 | tf_op jit(solution)/shard_map/all_gather | solution.py:105
  24.9 50.5 %reduce-scatter.2.cloned.1.call-start = ((), (), s32[]{:S(2)}) async-start(), calls=%async_computation.3 | async-start | bytes 393216 | tf_op jit(solution)/shard_map/reduce_scatter | solution.py:110
  56.6 161.2 %copy-start.7 = (s32[2,4]{1,0:T(2,128)S(1)}, s32[2,4]{1,0:T(2,128)}, u32[]{:S(2)}) copy-start(s32[2,4]{1,0:T(2,128)} %param.17) | copy-start | bytes 100
  63.5 167.5 %copy-start.6 = (pred[128,256]{0,1:T(8,128)(4,1)}, pred[128,256]{0,1:T(8,128)(4,1)S(1)}, u32[]{:S(2)}) copy-start(pred[128,256]{0,1:T(8,128)(4,1)S(1)} %fusion.37) | copy-start | bytes 98308
  76.4 142.5 %collective-permute-start = (bf16[2,128,256]{1,2,0:T(8,128)(2,1)S(1)}, bf16[2,128,256]{1,2,0:T(8,128)(2,1)S(1)}, u32[]{:S(2)}, u32[]{:S(2)}) collective-permute-start(bf16[2,128,256]{1,2,0:T(8,128)(2,1)S(1)} %copy.70), channel_id=1, source_target_pairs={{0,1},{2,3},{4,5},{6,7},{8,9},{10,11},{12,13},{14,15},{16,17},{18,... | collective-permute-start | bytes 393224 | tf_op jit(solution)/shard_map/ppermute | solution.py:17
  245.0 8.9 %copy-start.3 = (f32[2,8,128,128]{3,2,1,0:T(8,128)S(1)}, f32[2,8,128,128]{3,2,1,0:T(8,128)}, u32[]{:S(2)}) copy-start(f32[2,8,128,128]{3,2,1,0:T(8,128)} %get-tuple-element.201) | copy-start | bytes 3145732 | tf_op jit(solution)/shard_map/while
  249.1 5.8 %copy-start.2 = (f32[2,1024,128,8]{2,1,3,0:T(8,128)S(1)}, f32[2,1024,128,8]{2,1,3,0:T(8,128)}, u32[]{:S(2)}) copy-start(f32[2,1024,128,8]{2,1,3,0:T(8,128)} %get-tuple-element.185) | copy-start | bytes 25165828 | tf_op jit(solution)/shard_map/while
  258.4 1.0 copy-start.4
  261.4 8.9 %copy-start.3 = (f32[2,8,128,128]{3,2,1,0:T(8,128)S(1)}, f32[2,8,128,128]{3,2,1,0:T(8,128)}, u32[]{:S(2)}) copy-start(f32[2,8,128,128]{3,2,1,0:T(8,128)} %get-tuple-element.201) | copy-start | bytes 3145732 | tf_op jit(solution)/shard_map/while
  265.5 5.8 %copy-start.2 = (f32[2,1024,128,8]{2,1,3,0:T(8,128)S(1)}, f32[2,1024,128,8]{2,1,3,0:T(8,128)}, u32[]{:S(2)}) copy-start(f32[2,1024,128,8]{2,1,3,0:T(8,128)} %get-tuple-element.185) | copy-start | bytes 25165828 | tf_op jit(solution)/shard_map/while
  274.8 1.0 copy-start.4
  277.9 8.9 %copy-start.3 = (f32[2,8,128,128]{3,2,1,0:T(8,128)S(1)}, f32[2,8,128,128]{3,2,1,0:T(8,128)}, u32[]{:S(2)}) copy-start(f32[2,8,128,128]{3,2,1,0:T(8,128)} %get-tuple-element.201) | copy-start | bytes 3145732 | tf_op jit(solution)/shard_map/while
  282.0 5.8 %copy-start.2 = (f32[2,1024,128,8]{2,1,3,0:T(8,128)S(1)}, f32[2,1024,128,8]{2,1,3,0:T(8,128)}, u32[]{:S(2)}) copy-start(f32[2,1024,128,8]{2,1,3,0:T(8,128)} %get-tuple-element.185) | copy-start | bytes 25165828 | tf_op jit(solution)/shard_map/while
  291.2 1.0 copy-start.4
  294.3 8.9 %copy-start.3 = (f32[2,8,128,128]{3,2,1,0:T(8,128)S(1)}, f32[2,8,128,128]{3,2,1,0:T(8,128)}, u32[]{:S(2)}) copy-start(f32[2,8,128,128]{3,2,1,0:T(8,128)} %get-tuple-element.201) | copy-start | bytes 3145732 | tf_op jit(solution)/shard_map/while
  298.4 5.8 %copy-start.2 = (f32[2,1024,128,8]{2,1,3,0:T(8,128)S(1)}, f32[2,1024,128,8]{2,1,3,0:T(8,128)}, u32[]{:S(2)}) copy-start(f32[2,1024,128,8]{2,1,3,0:T(8,128)} %get-tuple-element.185) | copy-start | bytes 25165828 | tf_op jit(solution)/shard_map/while
  307.7 1.0 copy-start.4
  310.8 8.9 %copy-start.3 = (f32[2,8,128,128]{3,2,1,0:T(8,128)S(1)}, f32[2,8,128,128]{3,2,1,0:T(8,128)}, u32[]{:S(2)}) copy-start(f32[2,8,128,128]{3,2,1,0:T(8,128)} %get-tuple-element.201) | copy-start | bytes 3145732 | tf_op jit(solution)/shard_map/while
  314.8 5.8 %copy-start.2 = (f32[2,1024,128,8]{2,1,3,0:T(8,128)S(1)}, f32[2,1024,128,8]{2,1,3,0:T(8,128)}, u32[]{:S(2)}) copy-start(f32[2,1024,128,8]{2,1,3,0:T(8,128)} %get-tuple-element.185) | copy-start | bytes 25165828 | tf_op jit(solution)/shard_map/while
  324.1 1.0 copy-start.4
  327.2 8.9 %copy-start.3 = (f32[2,8,128,128]{3,2,1,0:T(8,128)S(1)}, f32[2,8,128,128]{3,2,1,0:T(8,128)}, u32[]{:S(2)}) copy-start(f32[2,8,128,128]{3,2,1,0:T(8,128)} %get-tuple-element.201) | copy-start | bytes 3145732 | tf_op jit(solution)/shard_map/while
  331.3 5.8 %copy-start.2 = (f32[2,1024,128,8]{2,1,3,0:T(8,128)S(1)}, f32[2,1024,128,8]{2,1,3,0:T(8,128)}, u32[]{:S(2)}) copy-start(f32[2,1024,128,8]{2,1,3,0:T(8,128)} %get-tuple-element.185) | copy-start | bytes 25165828 | tf_op jit(solution)/shard_map/while
  340.6 1.0 copy-start.4
  343.6 8.9 %copy-start.3 = (f32[2,8,128,128]{3,2,1,0:T(8,128)S(1)}, f32[2,8,128,128]{3,2,1,0:T(8,128)}, u32[]{:S(2)}) copy-start(f32[2,8,128,128]{3,2,1,0:T(8,128)} %get-tuple-element.201) | copy-start | bytes 3145732 | tf_op jit(solution)/shard_map/while
  347.7 5.8 %copy-start.2 = (f32[2,1024,128,8]{2,1,3,0:T(8,128)S(1)}, f32[2,1024,128,8]{2,1,3,0:T(8,128)}, u32[]{:S(2)}) copy-start(f32[2,1024,128,8]{2,1,3,0:T(8,128)} %get-tuple-element.185) | copy-start | bytes 25165828 | tf_op jit(solution)/shard_map/while
  357.0 1.0 copy-start.4
  360.1 8.9 %copy-start.3 = (f32[2,8,128,128]{3,2,1,0:T(8,128)S(1)}, f32[2,8,128,128]{3,2,1,0:T(8,128)}, u32[]{:S(2)}) copy-start(f32[2,8,128,128]{3,2,1,0:T(8,128)} %get-tuple-element.201) | copy-start | bytes 3145732 | tf_op jit(solution)/shard_map/while
  364.2 5.8 %copy-start.2 = (f32[2,1024,128,8]{2,1,3,0:T(8,128)S(1)}, f32[2,1024,128,8]{2,1,3,0:T(8,128)}, u32[]{:S(2)}) copy-start(f32[2,1024,128,8]{2,1,3,0:T(8,128)} %get-tuple-element.185) | copy-start | bytes 25165828 | tf_op jit(solution)/shard_map/while
  373.5 1.0 copy-start.4
  374.4 7.8 %copy-start.1 = (bf16[1,128,3584]{2,1,0:T(8,128)(2,1)S(1)}, bf16[1,128,3584]{2,1,0:T(8,128)(2,1)}, u32[]{:S(2)}) copy-start(bf16[1,128,3584]{2,1,0:T(8,128)(2,1)} %param.11) | copy-start | bytes 2752516
Sparse Core Ops, SparseCore 0:
  26.5 19.9 all-gather.1
  62.8 12.5 reduce-scatter.1
where the time goes:
time: 392 us; the launch traced here: 389 us
  blocking collectives  138 us (35%)
  local copies, waits for them, and re-layouts  80.2 us (20%)
  matrix products  70.5 us (18%)
  other arithmetic  46 us (12%)
  waiting for transfers between devices  32.3 us (8%)
  between operations  14.3 us (4%)
  starting transfers between devices  7.53 us (2%)
    all_gather x1, blocking collectives, shards(): spread = lax.all_gather(own_kv[None], 'store', axis=0, tiled=True)  138 us
    reduce_sum x9, other arithmetic, attend_block(): weight_sum = weight_sum * shrink + jnp.sum(weights, axis=-1)  40.2 us
    dot_general x9, matrix products, attend_block(): jnp.einsum('rhgd,khd->hgrk', query_matrix, key_rows, preferred_element_ty...  34.9 us
    dot_general x9, matrix products, attend_block(): jnp.einsum('hgrk,khd->hgrd', weights.astype(jnp.bfloat16), values, prefer...  29.9 us
    gather x2, local copies, waits for them, and re-layouts, receive_order(): return received[own_holders * capacity + my_rank]  20.8 us
    all_gather x1, waiting for transfers between devices, shards(): weight_full = lax.all_gather(key_value_weight, 'rep', axis=0, tiled=True)  19.7 us
    while x56, local copies, waits for them, and re-layouts  15.9 us
    dynamic_slice x24, local copies, waits for them, and re-layouts, scan_pages(): running, unused = lax.scan(visit_block, running, (page_blocks, ok_blocks))  15.9 us
  transfers between devices with their start and end apart: 4, of which 2 were waited for; matrix products, arithmetic and copies ran while one was open for 7% of the time, Pallas kernels for 0%

commit v1 on v0

--- a/solution.py
+++ b/solution.py
@@ -1,8 +1,11 @@
+import functools
 import math
 
 import jax
 import jax.numpy as jnp
 from jax import lax
+from jax.experimental import pallas as pl
+from jax.experimental.pallas import tpu as pltpu
 from jax.sharding import PartitionSpec as P
 
 HEAD_ENTRIES = 128
@@ -88,7 +91,7 @@
     return received[own_holders * capacity + my_rank]
 
 
-def shards(
+def pull_shards(
     queries, hidden, key_value_weight, page_store, prefix_holder, prefix_slot, prefix_len, new_owner
 ):
     store_id = lax.axis_index("store")
@@ -154,6 +157,393 @@
     return (result.astype(jnp.bfloat16), added_pages)
 
 
+MESH = pl.DeviceIdType.MESH
+SCORE_FACTOR = math.log2(math.e) / math.sqrt(HEAD_ENTRIES)
+KERNEL_BYTES = 60 * 2**20
+
+
+def held_table(holders, slots, lengths, capacity, page_len, store_id):
+    count = holders.shape[1]
+    place = jnp.arange(count, dtype=jnp.int32)
+    same = (holders[:, :, None] == holders[:, None, :]) & (place[None, None, :] < place[None, :, None])
+    ranking = jnp.sum(same.astype(jnp.int32), axis=-1)
+    chosen = (holders == store_id)[:, None, :] & (
+        ranking[:, None, :] == jnp.arange(capacity, dtype=jnp.int32)[None, :, None]
+    )
+    visible = jnp.clip(lengths[:, None] - place[None, :] * page_len, 0, page_len)
+    slot_of = jnp.sum(jnp.where(chosen, slots[:, None, :], 0), axis=-1)
+    visible_of = jnp.sum(jnp.where(chosen, visible[:, None, :], 0), axis=-1)
+    return jnp.stack([slot_of, visible_of])
+
+
+def merge(first, second):
+    out1, max1, sum1 = first
+    out2, max2, sum2 = second
+    top = jnp.maximum(max1, max2)
+    share1 = sum1 * jnp.exp2((max1 - top) * SCORE_FACTOR)
+    share2 = sum2 * jnp.exp2((max2 - top) * SCORE_FACTOR)
+    total = share1 + share2
+    inverse = 1.0 / jnp.maximum(total, 1.0)
+    return (out1 * (share1 * inverse) + out2 * (share2 * inverse), top, total)
+
+
+def attend_kernel(
+    stores, kv_heads, group_heads, capacity, tokens, page_len,
+    table, q_ref, pages, new_kv, out_ref,
+    q_buf, part, part_stat, inc, inc_stat, k_buf, v_buf,
+    q_send, q_recv, p_send, p_recv, t_send, t_recv,
+):
+    me = lax.axis_index("store")
+    rep_id = lax.axis_index("rep")
+    has_left = me > 0
+    has_right = me < stores - 1
+    entries = HEAD_ENTRIES
+    head_width = group_heads * entries
+
+    def q_copy(s, h, side):
+        step = 1 if side == 0 else -1
+        return pltpu.make_async_remote_copy(
+            src_ref=q_buf.at[s, h], dst_ref=q_buf.at[s, h],
+            send_sem=q_send.at[side, s, h], recv_sem=q_recv.at[s, h],
+            device_id={"store": me + step}, device_id_type=MESH,
+        )
+
+    def part_copies(s, h, side):
+        step = 1 if side == 0 else -1
+        return [
+            pltpu.make_async_remote_copy(
+                src_ref=source.at[s, h], dst_ref=target.at[side, s, h],
+                send_sem=send.at[s, h], recv_sem=recv.at[side, s, h],
+                device_id={"store": me + step}, device_id_type=MESH,
+            )
+            for source, target, send, recv in (
+                (part, inc, p_send, p_recv), (part_stat, inc_stat, t_send, t_recv)
+            )
+        ]
+
+    barrier = pltpu.get_barrier_semaphore()
+
+    @pl.when(has_left)
+    def _():
+        pl.semaphore_signal(barrier, inc=1, device_id={"store": me - 1}, device_id_type=MESH)
+
+    @pl.when(has_right)
+    def _():
+        pl.semaphore_signal(barrier, inc=1, device_id={"store": me + 1}, device_id_type=MESH)
+
+    for h in range(kv_heads):
+        q_buf[me, h] = q_ref[:, h * head_width:(h + 1) * head_width]
+
+    pl.semaphore_wait(barrier, has_left.astype(jnp.int32) + has_right.astype(jnp.int32))
+
+    def pass_query(s, h):
+        @pl.when((s <= me) & has_right)
+        def _():
+            q_copy(s, h, 0).start()
+
+        @pl.when((s >= me) & has_left)
+        def _():
+            q_copy(s, h, 1).start()
+
+    for h in range(kv_heads):
+        pass_query(me, h)
+
+    lane = lax.broadcasted_iota(jnp.int32, (tokens, entries), 1)
+
+    def softmax_block(scores, values):
+        top = jnp.max(scores, axis=1, keepdims=True)
+        weights = jnp.exp2((scores - top) * SCORE_FACTOR).astype(jnp.bfloat16)
+        return top, jnp.dot(weights, values, preferred_element_type=jnp.float32)
+
+    def compute(s, h):
+        columns = pl.ds(pl.multiple_of(h * entries, entries), entries)
+        spare = pages[table[0, s, 0], 0, 0:8, columns].astype(jnp.float32)[0:1]
+        row = lax.broadcasted_iota(jnp.int32, (page_len, entries), 0)
+
+        def lay(r, unused):
+            slot = table[0, s, r]
+            seen = row < table[1, s, r]
+            place = pl.ds(pl.multiple_of(r * page_len, page_len), page_len)
+            key = pages[slot, 0, :, columns].astype(jnp.float32)
+            value = pages[slot, 1, :, columns].astype(jnp.float32)
+            k_buf[place, :] = jnp.where(seen, key, spare).astype(jnp.bfloat16)
+            v_buf[place, 0:entries] = jnp.where(seen, value, 0.0).astype(jnp.bfloat16)
+            v_buf[place, entries:2 * entries] = jnp.where(seen, 1.0, 0.0).astype(jnp.bfloat16)
+            return unused
+
+        lax.fori_loop(0, capacity, lay, 0)
+        some = table[1, s, 0] > 0
+        stat = jnp.zeros((tokens, entries), jnp.float32)
+        for block in range(group_heads // 2):
+            at = block * 2 * entries
+            pair = q_buf[s, h, :, at:at + 2 * entries]
+            rows = jnp.concatenate([pair[:, :entries], pair[:, entries:]], axis=0)
+            scores = lax.dot_general(
+                rows, k_buf[...], (((1,), (1,)), ((), ())), preferred_element_type=jnp.float32
+            )
+            top, both = softmax_block(scores, v_buf[...])
+            weight_sum = both[:, entries:]
+            mean = (both[:, :entries] / jnp.maximum(weight_sum, 1.0)).astype(jnp.bfloat16)
+            top = jnp.where(some, top, NEG_FILL)
+            for k in range(2):
+                part[s, h, :, at + k * entries:at + (k + 1) * entries] = mean[k * tokens:(k + 1) * tokens]
+                head = 2 * block + k
+                stat = jnp.where(lane == head, top[k * tokens:(k + 1) * tokens], stat)
+                stat = jnp.where(lane == group_heads + head, weight_sum[k * tokens:(k + 1) * tokens], stat)
+        part_stat[s, h] = stat.T[0:2 * group_heads]
+
+    def unit(s, h):
+        compute(s, h)
+
+        @pl.when((s > me) & jnp.logical_not(has_left))
+        def _():
+            for copy in part_copies(s, h, 0):
+                copy.start()
+
+        @pl.when((s < me) & jnp.logical_not(has_right))
+        def _():
+            for copy in part_copies(s, h, 1):
+                copy.start()
+
+    def own(h, unused):
+        compute(me, h)
+        return unused
+
+    lax.fori_loop(0, kv_heads, own, 0)
+
+    def outward(index, unused):
+        distance = 1 + index // kv_heads
+        h = index % kv_heads
+        for s, inside in ((me - distance, me >= distance), (me + distance, me + distance < stores)):
+            @pl.when(inside)
+            def _():
+                q_copy(s, h, 0).wait_recv()
+                pass_query(s, h)
+
+        def each(turn, unused):
+            s = me + (2 * turn - 1) * distance
+
+            @pl.when((s >= 0) & (s < stores))
+            def _():
+                unit(s, h)
+
+            return unused
+
+        return lax.fori_loop(0, 2, each, unused)
+
+    lax.fori_loop(0, (stores - 1) * kv_heads, outward, 0)
+
+    def take_in(s, h, side):
+        for copy in part_copies(s, h, side):
+            copy.wait_recv()
+        mine = part_stat[s, h].T
+        theirs = inc_stat[side, s, h].T
+        stat = jnp.zeros((tokens, entries), jnp.float32)
+        for head in range(group_heads):
+            columns = slice(head * entries, (head + 1) * entries)
+
+            def state(where, numbers):
+                return (
+                    where[:, columns].astype(jnp.float32),
+                    jnp.broadcast_to(numbers[:, head:head + 1], (tokens, entries)),
+                    jnp.broadcast_to(numbers[:, group_heads + head:group_heads + head + 1], (tokens, entries)),
+                )
+
+            mean, top, total = merge(state(part.at[s, h], mine), state(inc.at[side, s, h], theirs))
+            part[s, h, :, columns] = mean.astype(jnp.bfloat16)
+            stat = jnp.where(lane == head, top, stat)
+            stat = jnp.where(lane == group_heads + head, total, stat)
+        part_stat[s, h] = stat.T[0:2 * group_heads]
+
+    key_index = lax.broadcasted_iota(jnp.int32, (2 * tokens, 2 * tokens), 1)
+    query_index = lax.broadcasted_iota(jnp.int32, (2 * tokens, 2 * tokens), 0) % tokens
+    allowed = (key_index - tokens <= query_index) & (key_index >= (1 - rep_id) * tokens)
+
+    def fresh(h, unused):
+        columns = pl.ds(pl.multiple_of(h * entries, entries), entries)
+        key = new_kv[0, :, columns]
+        value = jnp.concatenate(
+            [new_kv[1, :, columns], jnp.ones((2 * tokens, entries), jnp.bfloat16)], axis=1
+        )
+        mine = part_stat[me, h].T
+        stat = jnp.zeros((tokens, entries), jnp.float32)
+        for block in range(group_heads // 2):
+            at = block * 2 * entries
+            pair = q_buf[me, h, :, at:at + 2 * entries]
+            rows = jnp.concatenate([pair[:, :entries], pair[:, entries:]], axis=0)
+            scores = lax.dot_general(
+                rows, key, (((1,), (1,)), ((), ())), preferred_element_type=jnp.float32
+            )
+            top, both = softmax_block(jnp.where(allowed, scores, NEG_FILL), value)
+            for k in range(2):
+                head = 2 * block + k
+                columns_k = slice(at + k * entries, at + (k + 1) * entries)
+                span = slice(k * tokens, (k + 1) * tokens)
+                total = both[span, entries:]
+                mean, peak, total = merge(
+                    (both[span, :entries] / total, jnp.broadcast_to(top[span], (tokens, entries)), total),
+                    (
+                        part[me, h, :, columns_k].astype(jnp.float32),
+                        jnp.broadcast_to(mine[:, head:head + 1], (tokens, entries)),
+                        jnp.broadcast_to(mine[:, group_heads + head:group_heads + head + 1], (tokens, entries)),
+                    ),
+                )
+                part[me, h, :, columns_k] = mean.astype(jnp.bfloat16)
+                stat = jnp.where(lane == head, peak, stat)
+                stat = jnp.where(lane == group_heads + head, total, stat)
+        part_stat[me, h] = stat.T[0:2 * group_heads]
+        return unused
+
+    lax.fori_loop(0, kv_heads, fresh, 0)
+
+    def inward(index, unused):
+        distance = stores - 1 - index // kv_heads
+        h = index % kv_heads
+
+        @pl.when((me + distance < stores) & has_left)
+        def _():
+            take_in(me + distance, h, 0)
+            for copy in part_copies(me + distance, h, 0):
+                copy.start()
+
+        @pl.when((me >= distance) & has_right)
+        def _():
+            take_in(me - distance, h, 1)
+            for copy in part_copies(me - distance, h, 1):
+                copy.start()
+
+        return unused
+
+    lax.fori_loop(0, (stores - 1) * kv_heads, inward, 0)
+
+    def finish(h, unused):
+        @pl.when(has_left)
+        def _():
+            take_in(me, h, 0)
+
+        @pl.when(has_right)
+        def _():
+            take_in(me, h, 1)
+
+        width = pl.ds(pl.multiple_of(h * head_width, head_width), head_width)
+        out_ref[:, width] = part[me, h]
+        return unused
+
+    lax.fori_loop(0, kv_heads, finish, 0)
+
+    def drain(index, unused):
+        s = index // kv_heads
+        h = index % kv_heads
+
+        @pl.when((s <= me) & has_right)
+        def _():
+            q_copy(s, h, 0).wait_send()
+
+        @pl.when((s >= me) & has_left)
+        def _():
+            q_copy(s, h, 1).wait_send()
+
+        @pl.when(s != me)
+        def _():
+            for copy in part_copies(s, h, 0):
+                copy.wait_send()
+
+        return unused
+
+    lax.fori_loop(0, stores * kv_heads, drain, 0)
+
+
+def buffers_of(stores, kv_heads, group_heads, capacity, tokens, page_len):
+    head_width = group_heads * HEAD_ENTRIES
+    stat_rows = 2 * group_heads
+    return [
+        pltpu.VMEM((stores, kv_heads, tokens, head_width), jnp.bfloat16),
+        pltpu.VMEM((stores, kv_heads, tokens, head_width), jnp.bfloat16),
+        pltpu.VMEM((stores, kv_heads, stat_rows, tokens), jnp.float32),
+        pltpu.VMEM((2, stores, kv_heads, tokens, head_width), jnp.bfloat16),
+        pltpu.VMEM((2, stores, kv_heads, stat_rows, tokens), jnp.float32),
+        pltpu.VMEM((capacity * page_len, HEAD_ENTRIES), jnp.bfloat16),
+        pltpu.VMEM((capacity * page_len, 2 * HEAD_ENTRIES), jnp.bfloat16),
+        pltpu.SemaphoreType.DMA((2, stores, kv_heads)),
+        pltpu.SemaphoreType.DMA((stores, kv_heads)),
+        pltpu.SemaphoreType.DMA((stores, kv_heads)),
+        pltpu.SemaphoreType.DMA((2, stores, kv_heads)),
+        pltpu.SemaphoreType.DMA((stores, kv_heads)),
+        pltpu.SemaphoreType.DMA((2, stores, kv_heads)),
+    ]
+
+
+def attend(table, own_queries, page_store, new_kv, stores, kv_heads):
+    tokens = own_queries.shape[0]
+    page_len = page_store.shape[2]
+    group_heads = own_queries.shape[1] // (kv_heads * HEAD_ENTRIES)
+    capacity = table.shape[2]
+    sizes = (stores, kv_heads, group_heads, capacity, tokens, page_len)
+    vmem = pl.BlockSpec(memory_space=pltpu.VMEM)
+    pairs = stores * capacity * page_len * tokens * kv_heads * group_heads
+    return pl.pallas_call(
+        functools.partial(attend_kernel, *sizes),
+        out_shape=jax.ShapeDtypeStruct(own_queries.shape, jnp.bfloat16),
+        in_specs=[pl.BlockSpec(memory_space=pltpu.SMEM), vmem, vmem, vmem],
+        out_specs=vmem,
+        scratch_shapes=buffers_of(*sizes),
+        compiler_params=pltpu.CompilerParams(
+            collective_id=0, has_side_effects=True, vmem_limit_bytes=KERNEL_BYTES
+        ),
+        cost_estimate=pl.CostEstimate(
+            flops=4 * pairs * HEAD_ENTRIES, bytes_accessed=2 * page_store.size, transcendentals=pairs
+        ),
+        name="attend_pages",
+    )(table, own_queries, page_store, new_kv)
+
+
+def push_shards(
+    queries, hidden, key_value_weight, page_store, prefix_holder, prefix_slot, prefix_len, new_owner
+):
+    store_id = lax.axis_index("store")
+    rep_id = lax.axis_index("rep")
+    stores = lax.axis_size("store")
+    tensors = lax.axis_size("tensor")
+    tokens = queries.shape[1]
+    page_len = page_store.shape[2]
+    local_width = page_store.shape[3]
+    kv_heads = local_width // HEAD_ENTRIES
+    quarter_rows = hidden.shape[2]
+    list_len = prefix_slot.shape[1]
+    capacity = 2 * max(2, list_len // (2 * stores))
+    table = held_table(
+        prefix_holder[:, :, 0], prefix_slot, prefix_len, capacity, page_len, store_id
+    )
+    weight_full = lax.all_gather(key_value_weight, "rep", axis=0, tiled=True)
+    weight_five = weight_full.reshape(quarter_rows, tensors, kv_heads, 2, HEAD_ENTRIES)
+    partial_value = jnp.einsum(
+        "tc,cghkd->gkthd", hidden[0], weight_five, preferred_element_type=jnp.float32
+    )
+    summed = lax.psum_scatter(
+        partial_value.reshape(tensors * 2 * tokens, local_width).astype(jnp.bfloat16),
+        "tensor",
+        scatter_dimension=0,
+        tiled=True,
+    )
+    own_kv = summed.reshape(2, tokens, local_width)
+    spread = lax.all_gather(own_kv[None], "store", axis=0, tiled=True)
+    owner_row = lax.dynamic_index_in_dim(new_owner, rep_id, 0, keepdims=False)
+    source = jnp.argmax(owner_row == store_id)
+    new_page = lax.dynamic_index_in_dim(spread, source, 0, keepdims=False)
+    added_pages = new_page.reshape(1, 1, 2, tokens, local_width)
+    earlier = from_behind(own_kv, "rep", 1)
+    new_kv = jnp.concatenate([earlier, own_kv], axis=1)
+    attended = attend(table, queries[0], page_store, new_kv, stores, kv_heads)
+    return (attended[None], added_pages)
+
+
+def held_in_vmem(mesh, queries, page_store):
+    stores = mesh.shape["store"]
+    page_bytes = 2 * page_store.size // (mesh.shape["group"] * stores * mesh.shape["tensor"])
+    query_bytes = 2 * queries.size // (mesh.shape["group"] * mesh.shape["tensor"] * mesh.shape["rep"])
+    return page_bytes + 4 * query_bytes < KERNEL_BYTES // 2
+
+
 def solution(mesh):
     placed = (
         P(("group", "store"), "rep", "tensor"),
@@ -165,8 +555,8 @@
         P("group"),
         P(None, "group"),
     )
-    return jax.shard_map(
-        shards,
+    build = functools.partial(
+        jax.shard_map,
         mesh=mesh,
         in_specs=placed,
         out_specs=(
@@ -175,3 +565,9 @@
         ),
         check_vma=False,
     )
+
+    def whole(*arrays):
+        fits = held_in_vmem(mesh, arrays[0], arrays[3])
+        return build(push_shards if fits else pull_shards)(*arrays)
+
+    return whole

time: 392 us -> 158 us (0.40)
  blocking collectives: 138 us -> 16.1 us
  Pallas kernels: 0 us -> 69.6 us
  local copies, waits for them, and re-layouts: 80.2 us -> 13.6 us
  matrix products: 70.5 us -> 5.15 us
  other arithmetic: 46 us -> 5.55 us
  starting transfers between devices: 7.53 us -> 1.82 us
    all_gather x1, blocking collectives: 138 us -> 16.1 us  [push_shards(): spread = lax.all_gather(own_kv[None], 'store', axis=0, tiled=True)]
    pallas_call x0 -> x1, Pallas kernels: none -> 69.6 us  [attend(): pl.pallas_call(functools.partial(attend_kernel, *sizes), out_shape=jax.Sh...]
    dot_general x20 -> x1, matrix products: 70.5 us -> 5.15 us  [push_shards(): jnp.einsum('tc,cghkd->gkthd', hidden[0], weight_five, preferred_element_t...]
    reduce_sum x11 -> x2, other arithmetic: 41.9 us -> 1.2 us  [the longest x1 0.98 us: held_table(): ranking = jnp.sum(same.astype(jnp.int32), axis=-1)]
    gather x3 -> x0, local copies, waits for them, and re-layouts: 28.5 us -> none  [the longest x2 20.8 us: receive_order(): return received[own_holders * capacity + my_rank]]
    while x57 -> x0, local copies, waits for them, and re-layouts: 17.6 us -> none
    dynamic_slice x25 -> x0, local copies, waits for them, and re-layouts: 16.5 us -> none  [the longest x24 15.9 us: scan_pages(): running, unused = lax.scan(visit_block, running, (page_blocks, ok_blocks))]
    all_to_all x1 -> x0, starting transfers between devices: 5.72 us -> none  [shards(): lax.all_to_all(outgoing, 'store', split_axis=0, concat_axis=0, tiled=True)]
  transfers between devices with their start and end apart: 4 -> 3, of which waited for: 2 -> 2; matrix products, arithmetic and copies ran while one was open for 7% -> 3% of each run, Pallas kernels for 0% -> 0%
where the time goes in v1:
time: 158 us; the launch traced here: 157 us
  Pallas kernels  69.6 us (44%)
  waiting for transfers between devices  28.9 us (18%)
  blocking collectives  16.1 us (10%)
  between operations  16.1 us (10%)
  local copies, waits for them, and re-layouts  13.6 us (9%)
  other arithmetic  5.55 us (4%)
  matrix products  5.15 us (3%)
  starting transfers between devices  1.82 us (1%)
    pallas_call x1, Pallas kernels, attend(): pl.pallas_call(functools.partial(attend_kernel, *sizes), out_shape=jax.Sh...  69.6 us
    all_gather x1, waiting for transfers between devices, push_shards(): weight_full = lax.all_gather(key_value_weight, 'rep', axis=0, tiled=True)  16.4 us
    all_gather x1, blocking collectives, push_shards(): spread = lax.all_gather(own_kv[None], 'store', axis=0, tiled=True)  16.1 us
    reduce_scatter x1, waiting for transfers between devices, push_shards(): lax.psum_scatter(partial_value.reshape(tensors * 2 * tokens, local_width)...  11.8 us
    all_gather x1, local copies, waits for them, and re-layouts, push_shards(): weight_full = lax.all_gather(key_value_weight, 'rep', axis=0, tiled=True)  10.1 us
    dot_general x1, matrix products, push_shards(): jnp.einsum('tc,cghkd->gkthd', hidden[0], weight_five, preferred_element_t...  5.15 us
  transfers between devices with their start and end apart: 3, of which 2 were waited for; matrix products, arithmetic and copies ran while one was open for 3% of the time, Pallas kernels for 0%

profile of v1, /device:TPU:8, one launch (start us, length us, event | category | flops | bytes accessed | tf_op | source)
XLA Modules:
  0.0 156.8 jit_solution(5904082100492372410)
XLA Ops:
  7.2 0.0 copy-start
  7.2 0.0 all-gather.2.cloned.1.call-start
  7.2 0.7 all-gather.2.cloned.1.call-update
  7.9 0.0 reduce-scatter.2.cloned.1.call-start
  8.0 1.3 bitcast_reduce_fusion
  11.3 1.0 convert_reduce_fusion
  12.2 0.7 broadcast_compare_fusion
  12.9 16.4 %all-gather.2.cloned.1.call-done = bf16[3584,1024]{1,0:T(8,128)(2,1)} async-done(((bf16[1792,1024]{1,0:T(8,128)(2,1)}), bf16[3584,1024]{1,0:T(8,128)(2,1)}) %all-gather.2.cloned.1.call-update) | async-done | bytes 7340048 | tf_op jit(solution)/shard_map/all_gather | solution.py:517
  29.3 10.1 %copy.15 = bf16[3584,1024]{0,1:T(8,128)(2,1)} copy(bf16[3584,1024]{1,0:T(8,128)(2,1)} %all-gather.2.cloned.1.call-done) | data formatting | bytes 14680064 | tf_op jit(solution)/shard_map/all_gather | solution.py:517
  39.4 0.0 copy-start.2
  39.4 0.0 copy-start.1
  39.4 0.0 copy-done
  39.4 5.1 %fusion = bf16[2,2,128,2,128]{2,4,1,3,0:T(8,128)(2,1)S(1)} fusion(bf16[3584,2,2,2,128]{0,4,3,2,1:T(8,128)(2,1)} %bitcast.27, bf16[1,128,3584]{2,1,0:T(8,128)(2,1)S(1)} %copy-done), kind=kOutput, calls=%fused_computation.1 | convolution fusion | flops 939655168 | bytes 8519680 | tf_op jit(solution)/shard_map/tc,cghkd->gkthd/dot_general | solution.py:519
  44.6 0.2 copy.16
  44.7 0.7 copy.20
  45.5 0.0 reduce-scatter.2.cloned.1.call-update
  45.5 0.0 copy-done.2
  45.5 0.1 subtract_clamp_fusion
  45.6 0.0 copy-done.1
  45.6 0.2 select_reduce_fusion.1
  45.8 0.6 pad_add_fusion.table
  46.4 11.8 %reduce-scatter.2.cloned.1.call-done = bf16[256,256]{1,0:T(8,128)(2,1)} async-done(((bf16[512,256]{1,0:T(8,128)(2,1)}), bf16[256,256]{1,0:T(8,128)(2,1)}) %reduce-scatter.2.cloned.1.call-update) | async-done | bytes 131088 | tf_op jit(solution)/shard_map/reduce_scatter | solution.py:522
  58.2 1.7 %collective-permute-start = (bf16[2,128,256]{2,1,0:T(8,128)(2,1)}, bf16[2,128,256]{2,1,0:T(8,128)(2,1)S(1)}, u32[]{:S(2)}, u32[]{:S(2)}) collective-permute-start(bf16[2,128,256]{2,1,0:T(8,128)(2,1)} %bitcast.31), channel_id=1, source_target_pairs={{0,1},{2,3},{4,5},{6,7},{8,9},{10,11},{12,13},{14,15},{16,17},{18,... | collective-permute-start | bytes 393224 | tf_op jit(solution)/shard_map/ppermute | solution.py:20
  60.0 16.1 %all_gather.7 = bf16[4,2,128,256]{3,2,1,0:T(8,128)(2,1)S(1)} all-gather(bf16[1,2,128,256]{3,2,1,0:T(8,128)(2,1)} %bitcast.32), channel_id=1, replica_groups=mesh['group'=2,'store'=4,'tensor'=2,'rep'=2] {'store'}, dimensions={0}, use_global_device_ids=true | all-gather | bytes 655360 | tf_op jit(solution)/shard_map/all_gather | solution.py:529
  76.1 0.7 dynamic-slice_bitcast_fusion
  76.8 0.0 collective-permute-done
  76.8 1.6 %pad_maximum_fusion.new_kv = bf16[2,256,256]{2,1,0:T(8,128)(2,1)} fusion(bf16[2,128,256]{2,1,0:T(8,128)(2,1)} %bitcast.33, bf16[2,128,256]{2,1,0:T(8,128)(2,1)S(1)} %collective-permute-done), kind=kLoop, calls=%fused_computation.4 | loop fusion | flops 524288 | bytes 524288 | tf_op jit(solution)/shard_map/concatenate | solution.py:535
  78.4 69.6 %attend_pages.1 = bf16[128,2048]{1,0:T(8,128)(2,1)} custom-call(s32[2,4,16]{2,1,0:T(4,128)} %pad_add_fusion.table, bf16[128,2048]{1,0:T(8,128)(2,1)} %bitcast.38, bf16[32,2,128,256]{3,2,1,0:T(8,128)(2,1)} %pages.1, bf16[2,256,256]{2,1,0:T(8,128)(2,1)} %pad_maximum_fusion.new_kv), custom_call_target="tpu_custom_call" | custom-call | flops 8589934592 | bytes 4194304 | tf_op jit(solution)/shard_map/attend_pages/pallas_call | solution.py:484
  148.0 1.9 %copy.22 = bf16[1,128,2048]{2,1,0:T(8,128)(2,1)} copy(bf16[1,128,2048]{2,1,0:T(8,128)(2,1)} %bitcast.30) | data formatting | bytes 1048576
  (2 shorter events, 0.0 us)
Async XLA Ops:
  7.2 32.2 %copy-start = (bf16[1,128,3584]{2,1,0:T(8,128)(2,1)S(1)}, bf16[1,128,3584]{2,1,0:T(8,128)(2,1)}, u32[]{:S(2)}) copy-start(bf16[1,128,3584]{2,1,0:T(8,128)(2,1)} %param.9) | copy-start | bytes 2752516
  7.2 22.1 %all-gather.2.cloned.1.call-start = ((), (), s32[]{:S(2)}) async-start(), calls=%async_computation.1 | async-start | bytes 11010048 | tf_op jit(solution)/shard_map/all_gather | solution.py:517
  7.9 50.3 %reduce-scatter.2.cloned.1.call-start = ((), (), s32[]{:S(2)}) async-start(), calls=%async_computation.2 | async-start | bytes 393216 | tf_op jit(solution)/shard_map/reduce_scatter | solution.py:522
  39.4 6.1 %copy-start.2 = (s32[4]{0:T(128)S(1)}, s32[4]{0:T(128)}, u32[]{:S(2)}) copy-start(s32[4]{0:T(128)} %param.14) | copy-start | bytes 52
  39.4 6.2 %copy-start.1 = (s32[4,64]{1,0:T(4,128)S(1)}, s32[4,64]{1,0:T(4,128)}, u32[]{:S(2)}) copy-start(s32[4,64]{1,0:T(4,128)} %param.13) | copy-start | bytes 3076
  58.2 18.6 %collective-permute-start = (bf16[2,128,256]{2,1,0:T(8,128)(2,1)}, bf16[2,128,256]{2,1,0:T(8,128)(2,1)S(1)}, u32[]{:S(2)}, u32[]{:S(2)}) collective-permute-start(bf16[2,128,256]{2,1,0:T(8,128)(2,1)} %bitcast.31), channel_id=1, source_target_pairs={{0,1},{2,3},{4,5},{6,7},{8,9},{10,11},{12,13},{14,15},{16,17},{18,... | collective-permute-start | bytes 393224 | tf_op jit(solution)/shard_map/ppermute | solution.py:20
Sparse Core Ops, SparseCore 0:
  9.6 19.7 all-gather.1
  45.6 12.5 reduce-scatter.1

commit v2 on v1

--- a/solution.py
+++ b/solution.py
@@ -188,13 +188,21 @@
 
 
 def attend_kernel(
-    stores, kv_heads, group_heads, capacity, tokens, page_len,
-    table, q_ref, pages, new_kv, out_ref,
+    stores, tensors, kv_heads, group_heads, capacity, tokens, page_len,
+    table, source, q_ref, hidden, weight_hbm, pages_hbm, out_ref, added_ref,
     q_buf, part, part_stat, inc, inc_stat, k_buf, v_buf,
+    weight, pages, rows_in, products, terms, kv_buf, other_kv,
     q_send, q_recv, p_send, p_recv, t_send, t_recv,
+    load, rows_send, rows_recv, term_send, term_recv, kv_send, kv_recv, other_send, other_recv,
 ):
+    weight_load = pltpu.make_async_copy(weight_hbm, weight, load.at[0])
+    page_load = pltpu.make_async_copy(pages_hbm, pages, load.at[1])
+    page_load.start()
+    weight_load.start()
     me = lax.axis_index("store")
     rep_id = lax.axis_index("rep")
+    tensor_id = lax.axis_index("tensor")
+    other_rep = 1 - rep_id
     has_left = me > 0
     has_right = me < stores - 1
     entries = HEAD_ENTRIES
@@ -221,7 +229,50 @@
             )
         ]
 
+    depth = hidden.shape[1] // 2
+
+    def rows_copy():
+        return pltpu.make_async_remote_copy(
+            src_ref=hidden.at[:, pl.ds(pl.multiple_of(other_rep * depth, HEAD_ENTRIES), depth)],
+            dst_ref=rows_in.at[rep_id],
+            send_sem=rows_send, recv_sem=rows_recv,
+            device_id={"rep": other_rep}, device_id_type=MESH,
+        )
+
+    peers = [(dt, dr) for dt in range(tensors) for dr in range(2) if dt or dr]
+
+    def peer(dt, dr):
+        return lax.rem(tensor_id + dt, tensors), lax.rem(rep_id + dr, 2)
+
+    def term_copy(k):
+        tensor_to, rep_to = peer(*peers[k])
+        return pltpu.make_async_remote_copy(
+            src_ref=products.at[tensor_to, rep_to], dst_ref=terms.at[k],
+            send_sem=term_send.at[k], recv_sem=term_recv.at[k],
+            device_id={"tensor": tensor_to, "rep": rep_to}, device_id_type=MESH,
+        )
+
+    def kv_copy(s, side):
+        step = 1 if side == 0 else -1
+        return pltpu.make_async_remote_copy(
+            src_ref=kv_buf.at[s], dst_ref=kv_buf.at[s],
+            send_sem=kv_send.at[side, s], recv_sem=kv_recv.at[s],
+            device_id={"store": me + step}, device_id_type=MESH,
+        )
+
+    def other_copy():
+        return pltpu.make_async_remote_copy(
+            src_ref=kv_buf.at[me], dst_ref=other_kv,
+            send_sem=other_send, recv_sem=other_recv,
+            device_id={"rep": other_rep}, device_id_type=MESH,
+        )
+
     barrier = pltpu.get_barrier_semaphore()
+    for dt, dr in peers:
+        tensor_to, rep_to = peer(dt, dr)
+        pl.semaphore_signal(
+            barrier, inc=1, device_id={"tensor": tensor_to, "rep": rep_to}, device_id_type=MESH
+        )
 
     @pl.when(has_left)
     def _():
@@ -234,7 +285,8 @@
     for h in range(kv_heads):
         q_buf[me, h] = q_ref[:, h * head_width:(h + 1) * head_width]
 
-    pl.semaphore_wait(barrier, has_left.astype(jnp.int32) + has_right.astype(jnp.int32))
+    pl.semaphore_wait(barrier, has_left.astype(jnp.int32) + has_right.astype(jnp.int32) + len(peers))
+    rows_copy().start()
 
     def pass_query(s, h):
         @pl.when((s <= me) & has_right)
@@ -309,7 +361,54 @@
         compute(me, h)
         return unused
 
-    lax.fori_loop(0, kv_heads, own, 0)
+    page_load.wait()
+    lax.fori_loop(0, 1, own, 0)
+
+    rows_in[rep_id] = hidden[:, pl.ds(pl.multiple_of(rep_id * depth, entries), depth)]
+    rows_copy().wait_recv()
+    weight_load.wait()
+    all_rows = rows_in[...].reshape(2 * tokens, depth)
+    block_width = 2 * kv_heads * entries
+    for t in range(tensors):
+        product = jnp.dot(
+            all_rows, weight[:, t * block_width:(t + 1) * block_width],
+            preferred_element_type=jnp.float32,
+        ).astype(jnp.bfloat16)
+        for r in range(2):
+            products[t, r] = product[r * tokens:(r + 1) * tokens]
+    for k in range(len(peers)):
+        term_copy(k).start()
+
+    lax.fori_loop(1, kv_heads, own, 0)
+
+    total_kv = products[tensor_id, rep_id].astype(jnp.float32)
+    for k in range(len(peers)):
+        term_copy(k).wait_recv()
+        total_kv = total_kv + terms[k].astype(jnp.float32)
+    total_kv = total_kv.astype(jnp.bfloat16)
+    for head in range(kv_heads):
+        for kind in range(2):
+            at = (2 * head + kind) * entries
+            kv_buf[me, kind, :, head * entries:(head + 1) * entries] = total_kv[:, at:at + entries]
+
+    def pass_kv(s):
+        @pl.when((s <= me) & has_right)
+        def _():
+            kv_copy(s, 0).start()
+
+        @pl.when((s >= me) & has_left)
+        def _():
+            kv_copy(s, 1).start()
+
+    other_copy().start()
+    pass_kv(me)
+
+    def relay_kv(distance):
+        for s, inside in ((me - distance, me >= distance), (me + distance, me + distance < stores)):
+            @pl.when(inside)
+            def _():
+                kv_copy(s, 0).wait_recv()
+                pass_kv(s)
 
     def outward(index, unused):
         distance = 1 + index // kv_heads
@@ -329,9 +428,16 @@
 
             return unused
 
-        return lax.fori_loop(0, 2, each, unused)
+        unused = lax.fori_loop(0, 2, each, unused)
+
+        @pl.when((h == kv_heads - 1) & (distance > 1))
+        def _():
+            relay_kv(distance - 1)
+
+        return unused
 
     lax.fori_loop(0, (stores - 1) * kv_heads, outward, 0)
+    other_copy().wait_recv()
 
     def take_in(s, h, side):
         for copy in part_copies(s, h, side):
@@ -361,10 +467,9 @@
 
     def fresh(h, unused):
         columns = pl.ds(pl.multiple_of(h * entries, entries), entries)
-        key = new_kv[0, :, columns]
-        value = jnp.concatenate(
-            [new_kv[1, :, columns], jnp.ones((2 * tokens, entries), jnp.bfloat16)], axis=1
-        )
+        key = jnp.concatenate([other_kv[0, :, columns], kv_buf[me, 0, :, columns]], axis=0)
+        value = jnp.concatenate([other_kv[1, :, columns], kv_buf[me, 1, :, columns]], axis=0)
+        value = jnp.concatenate([value, jnp.ones((2 * tokens, entries), jnp.bfloat16)], axis=1)
         mine = part_stat[me, h].T
         stat = jnp.zeros((tokens, entries), jnp.float32)
         for block in range(group_heads // 2):
@@ -429,7 +534,26 @@
         out_ref[:, width] = part[me, h]
         return unused
 
+    relay_kv(stores - 1)
+    added_ref[...] = kv_buf[source[0]]
     lax.fori_loop(0, kv_heads, finish, 0)
+    rows_copy().wait_send()
+    for k in range(len(peers)):
+        term_copy(k).wait_send()
+    other_copy().wait_send()
+
+    def drain_kv(s, unused):
+        @pl.when((s <= me) & has_right)
+        def _():
+            kv_copy(s, 0).wait_send()
+
+        @pl.when((s >= me) & has_left)
+        def _():
+            kv_copy(s, 1).wait_send()
+
+        return unused
+
+    lax.fori_loop(0, stores, drain_kv, 0)
 
     def drain(index, unused):
         s = index // kv_heads
@@ -453,9 +577,10 @@
     lax.fori_loop(0, stores * kv_heads, drain, 0)
 
 
-def buffers_of(stores, kv_heads, group_heads, capacity, tokens, page_len):
+def buffers_of(stores, tensors, kv_heads, group_heads, capacity, tokens, page_len, weight, page_store):
     head_width = group_heads * HEAD_ENTRIES
     stat_rows = 2 * group_heads
+    block_width = 2 * kv_heads * HEAD_ENTRIES
     return [
         pltpu.VMEM((stores, kv_heads, tokens, head_width), jnp.bfloat16),
         pltpu.VMEM((stores, kv_heads, tokens, head_width), jnp.bfloat16),
@@ -464,29 +589,50 @@
         pltpu.VMEM((2, stores, kv_heads, stat_rows, tokens), jnp.float32),
         pltpu.VMEM((capacity * page_len, HEAD_ENTRIES), jnp.bfloat16),
         pltpu.VMEM((capacity * page_len, 2 * HEAD_ENTRIES), jnp.bfloat16),
+        pltpu.VMEM(weight.shape, weight.dtype),
+        pltpu.VMEM(page_store.shape, page_store.dtype),
+        pltpu.VMEM((2, tokens, weight.shape[0]), jnp.bfloat16),
+        pltpu.VMEM((tensors, 2, tokens, block_width), jnp.bfloat16),
+        pltpu.VMEM((2 * tensors - 1, tokens, block_width), jnp.bfloat16),
+        pltpu.VMEM((stores, 2, tokens, block_width // 2), jnp.bfloat16),
+        pltpu.VMEM((2, tokens, block_width // 2), jnp.bfloat16),
         pltpu.SemaphoreType.DMA((2, stores, kv_heads)),
         pltpu.SemaphoreType.DMA((stores, kv_heads)),
         pltpu.SemaphoreType.DMA((stores, kv_heads)),
         pltpu.SemaphoreType.DMA((2, stores, kv_heads)),
         pltpu.SemaphoreType.DMA((stores, kv_heads)),
         pltpu.SemaphoreType.DMA((2, stores, kv_heads)),
+        pltpu.SemaphoreType.DMA((2,)),
+        pltpu.SemaphoreType.DMA,
+        pltpu.SemaphoreType.DMA,
+        pltpu.SemaphoreType.DMA((2 * tensors - 1,)),
+        pltpu.SemaphoreType.DMA((2 * tensors - 1,)),
+        pltpu.SemaphoreType.DMA((2, stores)),
+        pltpu.SemaphoreType.DMA((stores,)),
+        pltpu.SemaphoreType.DMA,
+        pltpu.SemaphoreType.DMA,
     ]
 
 
-def attend(table, own_queries, page_store, new_kv, stores, kv_heads):
+def attend(table, source, own_queries, own_rows, weight, page_store, stores, tensors, kv_heads):
     tokens = own_queries.shape[0]
     page_len = page_store.shape[2]
     group_heads = own_queries.shape[1] // (kv_heads * HEAD_ENTRIES)
     capacity = table.shape[2]
-    sizes = (stores, kv_heads, group_heads, capacity, tokens, page_len)
+    sizes = (stores, tensors, kv_heads, group_heads, capacity, tokens, page_len)
+    smem = pl.BlockSpec(memory_space=pltpu.SMEM)
     vmem = pl.BlockSpec(memory_space=pltpu.VMEM)
+    where_it_is = pl.BlockSpec(memory_space=pl.ANY)
     pairs = stores * capacity * page_len * tokens * kv_heads * group_heads
     return pl.pallas_call(
         functools.partial(attend_kernel, *sizes),
-        out_shape=jax.ShapeDtypeStruct(own_queries.shape, jnp.bfloat16),
-        in_specs=[pl.BlockSpec(memory_space=pltpu.SMEM), vmem, vmem, vmem],
-        out_specs=vmem,
-        scratch_shapes=buffers_of(*sizes),
+        out_shape=(
+            jax.ShapeDtypeStruct(own_queries.shape, jnp.bfloat16),
+            jax.ShapeDtypeStruct((2, tokens, kv_heads * HEAD_ENTRIES), jnp.bfloat16),
+        ),
+        in_specs=[smem, smem, vmem, vmem, where_it_is, where_it_is],
+        out_specs=(vmem, vmem),
+        scratch_shapes=buffers_of(*sizes, weight, page_store),
         compiler_params=pltpu.CompilerParams(
             collective_id=0, has_side_effects=True, vmem_limit_bytes=KERNEL_BYTES
         ),
@@ -494,7 +640,7 @@
             flops=4 * pairs * HEAD_ENTRIES, bytes_accessed=2 * page_store.size, transcendentals=pairs
         ),
         name="attend_pages",
-    )(table, own_queries, page_store, new_kv)
+    )(table, source, own_queries, own_rows, weight, page_store)
 
 
 def push_shards(
@@ -504,37 +650,20 @@
     rep_id = lax.axis_index("rep")
     stores = lax.axis_size("store")
     tensors = lax.axis_size("tensor")
-    tokens = queries.shape[1]
     page_len = page_store.shape[2]
-    local_width = page_store.shape[3]
-    kv_heads = local_width // HEAD_ENTRIES
-    quarter_rows = hidden.shape[2]
+    kv_heads = page_store.shape[3] // HEAD_ENTRIES
     list_len = prefix_slot.shape[1]
     capacity = 2 * max(2, list_len // (2 * stores))
     table = held_table(
         prefix_holder[:, :, 0], prefix_slot, prefix_len, capacity, page_len, store_id
     )
-    weight_full = lax.all_gather(key_value_weight, "rep", axis=0, tiled=True)
-    weight_five = weight_full.reshape(quarter_rows, tensors, kv_heads, 2, HEAD_ENTRIES)
-    partial_value = jnp.einsum(
-        "tc,cghkd->gkthd", hidden[0], weight_five, preferred_element_type=jnp.float32
-    )
-    summed = lax.psum_scatter(
-        partial_value.reshape(tensors * 2 * tokens, local_width).astype(jnp.bfloat16),
-        "tensor",
-        scatter_dimension=0,
-        tiled=True,
-    )
-    own_kv = summed.reshape(2, tokens, local_width)
-    spread = lax.all_gather(own_kv[None], "store", axis=0, tiled=True)
     owner_row = lax.dynamic_index_in_dim(new_owner, rep_id, 0, keepdims=False)
-    source = jnp.argmax(owner_row == store_id)
-    new_page = lax.dynamic_index_in_dim(spread, source, 0, keepdims=False)
-    added_pages = new_page.reshape(1, 1, 2, tokens, local_width)
-    earlier = from_behind(own_kv, "rep", 1)
-    new_kv = jnp.concatenate([earlier, own_kv], axis=1)
-    attended = attend(table, queries[0], page_store, new_kv, stores, kv_heads)
-    return (attended[None], added_pages)
+    request = jnp.arange(stores, dtype=jnp.int32)
+    source = jnp.sum(jnp.where(owner_row == store_id, request, 0), keepdims=True)
+    attended, added = attend(
+        table, source, queries[0], hidden[0], key_value_weight, page_store, stores, tensors, kv_heads
+    )
+    return (attended[None], added[None, None])
 
 
 def held_in_vmem(mesh, queries, page_store):

time: 158 us -> 91 us (0.58)
  waiting for transfers between devices: 28.9 us -> 0 us
  blocking collectives: 16.1 us -> 0 us
  between operations: 16.1 us -> 0.65 us
  Pallas kernels: 69.6 us -> 81.3 us
  local copies, waits for them, and re-layouts: 13.6 us -> 3.45 us
  matrix products: 5.15 us -> 0 us
  starting transfers between devices: 1.82 us -> 0 us
    all_gather x1 -> x0, waiting for transfers between devices: 16.4 us -> none  [push_shards(): weight_full = lax.all_gather(key_value_weight, 'rep', axis=0, tiled=True)]
    all_gather x1 -> x0, blocking collectives: 16.1 us -> none  [push_shards(): spread = lax.all_gather(own_kv[None], 'store', axis=0, tiled=True)]
    reduce_scatter x1 -> x0, waiting for transfers between devices: 11.8 us -> none  [push_shards(): lax.psum_scatter(partial_value.reshape(tensors * 2 * tokens, local_width)...]
    pallas_call x1, Pallas kernels: 69.6 us -> 81.3 us  [attend(): pl.pallas_call(functools.partial(attend_kernel, *sizes), out_shape=(jax.S...]
    all_gather x1 -> x0, local copies, waits for them, and re-layouts: 10.1 us -> none  [push_shards(): weight_full = lax.all_gather(key_value_weight, 'rep', axis=0, tiled=True)]
    dot_general x1 -> x0, matrix products: 5.15 us -> none  [push_shards(): jnp.einsum('tc,cghkd->gkthd', hidden[0], weight_five, preferred_element_t...]
    ppermute x1 -> x0, starting transfers between devices: 1.75 us -> none  [from_behind(): return lax.ppermute(block, axis, route)]
    concatenate x1 -> x0, other arithmetic: 1.62 us -> none  [push_shards(): new_kv = jnp.concatenate([earlier, own_kv], axis=1)]
  transfers between devices with their start and end apart: 3 -> 0, of which waited for: 2 -> 0; matrix products, arithmetic and copies ran while one was open for 3% -> 0% of each run, Pallas kernels for 0% -> 0%
where the time goes in v2:
time: 91 us; the launch traced here: 90.7 us
  Pallas kernels  81.3 us (89%)
  other arithmetic  5.24 us (6%)
  local copies, waits for them, and re-layouts  3.45 us (4%)
    pallas_call x1, Pallas kernels, attend(): pl.pallas_call(functools.partial(attend_kernel, *sizes), out_shape=(jax.S...  81.3 us
    unnamed x2, local copies, waits for them, and re-layouts  3.45 us

profile of v2, /device:TPU:8, one launch (start us, length us, event | category | flops | bytes accessed | tf_op | source)
XLA Modules:
  0.0 90.7 jit_solution(13713164461644337930)
XLA Ops:
  0.6 1.3 %fusion.1 = s32[]{:T(128)} fusion(s32[2,4]{1,0:T(2,128)} %param.15, s32[]{:T(128)S(6)} %select_n.17, s32[]{:T(128)S(6)} %axis_index.23), kind=kLoop, calls=%fused_computation.10 | loop fusion | flops 11 | bytes 28 | tf_op jit(solution)/shard_map/reduce_sum | solution.py:662
  2.0 0.7 broadcast_compare_fusion
  2.6 0.7 subtract_clamp_fusion
  3.4 1.0 %convert_reduce_fusion = s32[4,64]{1,0:T(4,128)S(1)} fusion(s32[4,64]{1,0:T(4,128)} %bitcast.15, pred[64,64]{1,0:T(8,128)(4,1)S(1)} %iota_compare_fusion.1), kind=kLoop, calls=%fused_computation | loop fusion | flops 65280 | bytes 6144 | tf_op jit(solution)/shard_map/reduce_sum | solution.py:169
  4.4 0.9 select_reduce_fusion.1
  5.3 0.6 pad_add_fusion.table
  5.9 81.3 %attend_pages.1 = (bf16[128,2048]{1,0:T(8,128)(2,1)}, bf16[2,128,256]{2,1,0:T(8,128)(2,1)}) custom-call(s32[2,4,16]{2,1,0:T(4,128)} %pad_add_fusion.table, s32[1]{0:T(128)} %bitcast.4.source, bf16[128,2048]{1,0:T(8,128)(2,1)} %bitcast.19, bf16[128,3584]{1,0:T(8,128)(2,1)} %bitcast.18, bf16[1792,1024]{1,0:T(8,128)(2,1)} %weight_hbm.1, ...), custom_call_target="tpu_custom_call" | custom-call | flops 8589934592 | bytes 4194304 | tf_op jit(solution)/shard_map/attend_pages/pallas_call | solution.py:627
  87.2 1.9 %copy.12 = bf16[1,128,2048]{2,1,0:T(8,128)(2,1)} copy(bf16[1,128,2048]{2,1,0:T(8,128)(2,1)} %bitcast.12) | data formatting | bytes 1048576
  89.1 1.6 %copy.13 = bf16[1,1,2,128,256]{4,3,2,1,0:T(8,128)(2,1)} copy(bf16[1,1,2,128,256]{4,3,2,1,0:T(8,128)(2,1)} %bitcast.13) | data formatting | bytes 262144
  (2 shorter events, 0.0 us)

commit v3 on v2

--- a/solution.py
+++ b/solution.py
@@ -162,7 +162,7 @@
 KERNEL_BYTES = 60 * 2**20
 
 
-def held_table(holders, slots, lengths, capacity, page_len, store_id):
+def held_table(holders, slots, capacity, store_id):
     count = holders.shape[1]
     place = jnp.arange(count, dtype=jnp.int32)
     same = (holders[:, :, None] == holders[:, None, :]) & (place[None, None, :] < place[None, :, None])
@@ -170,10 +170,8 @@
     chosen = (holders == store_id)[:, None, :] & (
         ranking[:, None, :] == jnp.arange(capacity, dtype=jnp.int32)[None, :, None]
     )
-    visible = jnp.clip(lengths[:, None] - place[None, :] * page_len, 0, page_len)
-    slot_of = jnp.sum(jnp.where(chosen, slots[:, None, :], 0), axis=-1)
-    visible_of = jnp.sum(jnp.where(chosen, visible[:, None, :], 0), axis=-1)
-    return jnp.stack([slot_of, visible_of])
+    entry = slots * count + place[None, :] + 1
+    return jnp.sum(jnp.where(chosen, entry[:, None, :], 0), axis=-1)
 
 
 def merge(first, second):
@@ -188,8 +186,8 @@
 
 
 def attend_kernel(
-    stores, tensors, kv_heads, group_heads, capacity, tokens, page_len,
-    table, source, q_ref, hidden, weight_hbm, pages_hbm, out_ref, added_ref,
+    list_len, stores, tensors, kv_heads, group_heads, capacity, tokens, page_len,
+    table, lengths, new_owner, q_ref, hidden, weight_hbm, pages_hbm, out_ref, added_ref,
     q_buf, part, part_stat, inc, inc_stat, k_buf, v_buf,
     weight, pages, rows_in, products, terms, kv_buf, other_kv,
     q_send, q_recv, p_send, p_recv, t_send, t_recv,
@@ -309,12 +307,20 @@
 
     def compute(s, h):
         columns = pl.ds(pl.multiple_of(h * entries, entries), entries)
-        spare = pages[table[0, s, 0], 0, 0:8, columns].astype(jnp.float32)[0:1]
+
+        def listed(r):
+            entry = table[s, r]
+            place = jnp.maximum(entry - 1, 0)
+            seen = lengths[s] - lax.rem(place, list_len) * page_len
+            return lax.div(place, list_len), jnp.where(entry > 0, seen, 0)
+
+        first, first_seen = listed(0)
+        spare = pages[first, 0, 0:8, columns].astype(jnp.float32)[0:1]
         row = lax.broadcasted_iota(jnp.int32, (page_len, entries), 0)
 
         def lay(r, unused):
-            slot = table[0, s, r]
-            seen = row < table[1, s, r]
+            slot, seen_rows = listed(r)
+            seen = row < seen_rows
             place = pl.ds(pl.multiple_of(r * page_len, page_len), page_len)
             key = pages[slot, 0, :, columns].astype(jnp.float32)
             value = pages[slot, 1, :, columns].astype(jnp.float32)
@@ -324,15 +330,23 @@
             return unused
 
         lax.fori_loop(0, capacity, lay, 0)
-        some = table[1, s, 0] > 0
+        some = first_seen > 0
         stat = jnp.zeros((tokens, entries), jnp.float32)
-        for block in range(group_heads // 2):
-            at = block * 2 * entries
-            pair = q_buf[s, h, :, at:at + 2 * entries]
+
+        def score(block):
+            pair = q_buf[s, h, :, block * 2 * entries:(block + 1) * 2 * entries]
             rows = jnp.concatenate([pair[:, :entries], pair[:, entries:]], axis=0)
-            scores = lax.dot_general(
+            return lax.dot_general(
                 rows, k_buf[...], (((1,), (1,)), ((), ())), preferred_element_type=jnp.float32
             )
+
+        blocks = group_heads // 2
+        upcoming = score(0)
+        for block in range(blocks):
+            at = block * 2 * entries
+            scores = upcoming
+            if block + 1 < blocks:
+                upcoming = score(block + 1)
             top, both = softmax_block(scores, v_buf[...])
             weight_sum = both[:, entries:]
             mean = (both[:, :entries] / jnp.maximum(weight_sum, 1.0)).astype(jnp.bfloat16)
@@ -379,18 +393,6 @@
     for k in range(len(peers)):
         term_copy(k).start()
 
-    lax.fori_loop(1, kv_heads, own, 0)
-
-    total_kv = products[tensor_id, rep_id].astype(jnp.float32)
-    for k in range(len(peers)):
-        term_copy(k).wait_recv()
-        total_kv = total_kv + terms[k].astype(jnp.float32)
-    total_kv = total_kv.astype(jnp.bfloat16)
-    for head in range(kv_heads):
-        for kind in range(2):
-            at = (2 * head + kind) * entries
-            kv_buf[me, kind, :, head * entries:(head + 1) * entries] = total_kv[:, at:at + entries]
-
     def pass_kv(s):
         @pl.when((s <= me) & has_right)
         def _():
@@ -400,8 +402,18 @@
         def _():
             kv_copy(s, 1).start()
 
-    other_copy().start()
-    pass_kv(me)
+    def own_pages():
+        total_kv = products[tensor_id, rep_id].astype(jnp.float32)
+        for k in range(len(peers)):
+            term_copy(k).wait_recv()
+            total_kv = total_kv + terms[k].astype(jnp.float32)
+        total_kv = total_kv.astype(jnp.bfloat16)
+        for head in range(kv_heads):
+            for kind in range(2):
+                at = (2 * head + kind) * entries
+                kv_buf[me, kind, :, head * entries:(head + 1) * entries] = total_kv[:, at:at + entries]
+        other_copy().start()
+        pass_kv(me)
 
     def relay_kv(distance):
         for s, inside in ((me - distance, me >= distance), (me + distance, me + distance < stores)):
@@ -429,6 +441,7 @@
             return unused
 
         unused = lax.fori_loop(0, 2, each, unused)
+        pl.when(index == 0)(own_pages)
 
         @pl.when((h == kv_heads - 1) & (distance > 1))
         def _():
@@ -438,6 +451,8 @@
 
     lax.fori_loop(0, (stores - 1) * kv_heads, outward, 0)
     other_copy().wait_recv()
+    at_end = jnp.logical_not(has_left & has_right)
+    lax.fori_loop(jnp.where(at_end, 1, kv_heads), kv_heads, own, 0)
 
     def take_in(s, h, side):
         for copy in part_copies(s, h, side):
@@ -499,8 +514,6 @@
         part_stat[me, h] = stat.T[0:2 * group_heads]
         return unused
 
-    lax.fori_loop(0, kv_heads, fresh, 0)
-
     def inward(index, unused):
         distance = stores - 1 - index // kv_heads
         h = index % kv_heads
@@ -520,6 +533,8 @@
         return unused
 
     lax.fori_loop(0, (stores - 1) * kv_heads, inward, 0)
+    lax.fori_loop(jnp.where(at_end, kv_heads, 1), kv_heads, own, 0)
+    lax.fori_loop(0, kv_heads, fresh, 0)
 
     def finish(h, unused):
         @pl.when(has_left)
@@ -535,7 +550,10 @@
         return unused
 
     relay_kv(stores - 1)
-    added_ref[...] = kv_buf[source[0]]
+    source = 0
+    for s in range(1, stores):
+        source = jnp.where(new_owner[rep_id, s] == me, s, source)
+    added_ref[...] = kv_buf[source]
     lax.fori_loop(0, kv_heads, finish, 0)
     rows_copy().wait_send()
     for k in range(len(peers)):
@@ -614,23 +632,26 @@
     ]
 
 
-def attend(table, source, own_queries, own_rows, weight, page_store, stores, tensors, kv_heads):
+def attend(
+    table, lengths, new_owner, own_queries, own_rows, weight, page_store,
+    list_len, stores, tensors, kv_heads,
+):
     tokens = own_queries.shape[0]
     page_len = page_store.shape[2]
     group_heads = own_queries.shape[1] // (kv_heads * HEAD_ENTRIES)
-    capacity = table.shape[2]
+    capacity = table.shape[1]
     sizes = (stores, tensors, kv_heads, group_heads, capacity, tokens, page_len)
     smem = pl.BlockSpec(memory_space=pltpu.SMEM)
     vmem = pl.BlockSpec(memory_space=pltpu.VMEM)
     where_it_is = pl.BlockSpec(memory_space=pl.ANY)
     pairs = stores * capacity * page_len * tokens * kv_heads * group_heads
     return pl.pallas_call(
-        functools.partial(attend_kernel, *sizes),
+        functools.partial(attend_kernel, list_len, *sizes),
         out_shape=(
             jax.ShapeDtypeStruct(own_queries.shape, jnp.bfloat16),
             jax.ShapeDtypeStruct((2, tokens, kv_heads * HEAD_ENTRIES), jnp.bfloat16),
         ),
-        in_specs=[smem, smem, vmem, vmem, where_it_is, where_it_is],
+        in_specs=[smem, smem, smem, vmem, vmem, where_it_is, where_it_is],
         out_specs=(vmem, vmem),
         scratch_shapes=buffers_of(*sizes, weight, page_store),
         compiler_params=pltpu.CompilerParams(
@@ -640,28 +661,22 @@
             flops=4 * pairs * HEAD_ENTRIES, bytes_accessed=2 * page_store.size, transcendentals=pairs
         ),
         name="attend_pages",
-    )(table, source, own_queries, own_rows, weight, page_store)
+    )(table, lengths, new_owner, own_queries, own_rows, weight, page_store)
 
 
 def push_shards(
     queries, hidden, key_value_weight, page_store, prefix_holder, prefix_slot, prefix_len, new_owner
 ):
     store_id = lax.axis_index("store")
-    rep_id = lax.axis_index("rep")
     stores = lax.axis_size("store")
     tensors = lax.axis_size("tensor")
-    page_len = page_store.shape[2]
     kv_heads = page_store.shape[3] // HEAD_ENTRIES
     list_len = prefix_slot.shape[1]
     capacity = 2 * max(2, list_len // (2 * stores))
-    table = held_table(
-        prefix_holder[:, :, 0], prefix_slot, prefix_len, capacity, page_len, store_id
-    )
-    owner_row = lax.dynamic_index_in_dim(new_owner, rep_id, 0, keepdims=False)
-    request = jnp.arange(stores, dtype=jnp.int32)
-    source = jnp.sum(jnp.where(owner_row == store_id, request, 0), keepdims=True)
+    table = held_table(prefix_holder[:, :, 0], prefix_slot, capacity, store_id)
     attended, added = attend(
-        table, source, queries[0], hidden[0], key_value_weight, page_store, stores, tensors, kv_heads
+        table, prefix_len, new_owner, queries[0], hidden[0], key_value_weight, page_store,
+        list_len, stores, tensors, kv_heads,
     )
     return (attended[None], added[None, None])
 

time: 91 us -> 84.7 us (0.931)
  Pallas kernels: 81.3 us -> 77.2 us
  other arithmetic: 5.24 us -> 3.1 us
    pallas_call x1, Pallas kernels: 81.3 us -> 77.2 us  [attend(): pl.pallas_call(functools.partial(attend_kernel, list_len, *sizes), out_sh...]
    reduce_sum x2 -> x1, other arithmetic: 2.23 us -> 0.74 us  [held_table(): return jnp.sum(jnp.where(chosen, entry[:, None, :], 0), axis=-1)]
where the time goes in v3:
time: 84.7 us; the launch traced here: 84.4 us
  Pallas kernels  77.2 us (91%)
  local copies, waits for them, and re-layouts  3.45 us (4%)
  other arithmetic  3.1 us (4%)
    pallas_call x1, Pallas kernels, attend(): pl.pallas_call(functools.partial(attend_kernel, list_len, *sizes), out_sh...  77.2 us
    unnamed x2, local copies, waits for them, and re-layouts  3.45 us

profile of v3, /device:TPU:8, one launch (start us, length us, event | category | flops | bytes accessed | tf_op | source)
XLA Modules:
  0.0 84.4 jit_solution(575416524941030532)
XLA Ops:
  0.6 0.7 broadcast_compare_fusion
  1.3 0.7 add_add_fusion
  2.0 1.0 %convert_reduce_fusion = s32[4,64]{1,0:T(4,128)S(1)} fusion(s32[4,64]{1,0:T(4,128)} %bitcast.8, pred[64,64]{1,0:T(8,128)(4,1)S(1)} %iota_compare_fusion.1), kind=kLoop, calls=%fused_computation | loop fusion | flops 65280 | bytes 6144 | tf_op jit(solution)/shard_map/reduce_sum | solution.py:169
  3.0 0.7 select_reduce_fusion.table
  3.7 77.2 %attend_pages.1 = (bf16[128,2048]{1,0:T(8,128)(2,1)}, bf16[2,128,256]{2,1,0:T(8,128)(2,1)}) custom-call(s32[4,16]{1,0:T(4,128)} %select_reduce_fusion.table, s32[4]{0:T(128)} %lengths.1, s32[2,4]{1,0:T(2,128)} %new_owner.1, bf16[128,2048]{1,0:T(8,128)(2,1)} %bitcast.10, bf16[128,3584]{1,0:T(8,128)(2,1)} %bitcast.9, bf16[1792,1024]{1,0:T(8,128)(2,1)} %weight_hbm.1, ...), custom_call_target="tpu_custom_call" | custom-call | flops 8589934592 | bytes 4194304 | tf_op jit(solution)/shard_map/attend_pages/pallas_call | solution.py:648
  80.9 1.9 %copy.12 = bf16[1,128,2048]{2,1,0:T(8,128)(2,1)} copy(bf16[1,128,2048]{2,1,0:T(8,128)(2,1)} %bitcast.5) | data formatting | bytes 1048576
  82.8 1.6 %copy.13 = bf16[1,1,2,128,256]{4,3,2,1,0:T(8,128)(2,1)} copy(bf16[1,1,2,128,256]{4,3,2,1,0:T(8,128)(2,1)} %bitcast.6) | data formatting | bytes 262144
  (1 shorter events, 0.0 us)
